TPU v7x, 256 devices: a whole 4x4x8 slice. The times are simulated.
256 devices in a mesh: ctx: 32 (over y, x, core), tp: 8 (over z).
Axes of the slice: x: 4, y: 4, z: 8, core: 2. Of those that a mesh axis runs over, the one named last changes fastest.
Arguments:
- x_raw: bfloat16 [49152, 8192], P('ctx', 'tp'), may hold values from -6 to 6
- bc_raw: bfloat16 [49152, 256], P('ctx'), may hold values from -6 to 6
- z_gate: bfloat16 [49152, 8192], P('ctx', 'tp'), may hold values from -6 to 6
- conv_x: float32 [4, 8192], P(None, 'tp'), may hold values from -3 to 3
- conv_bc: float32 [4, 256], replicated, may hold values from -3 to 3
- step_size: float32 [49152, 128], P('ctx', 'tp'), may hold values from 0.0007 to 0.063, as said below
- log_decay: float32 [49152, 128], P('ctx', 'tp'), may hold values from -0.62 to 0, as said below
- skip_scale: float32 [128], P('tp'), may hold values from 0.5 to 3, as said below
- norm_gain: float32 [8192], P('tp'), may hold values from 0.5 to 1.5
Outputs:
- layer_out: bfloat16 [49152, 8192], P('ctx', 'tp')
Inputs may be any that keep to these rules, and one draw needn't show every extreme that they name: `step_size`: positive step sizes. `log_decay`: each entry is negative; exp of it is the factor by which the head's state is kept from the previous token. `skip_scale`: positive coefficients.
All inputs are finite; a program needn't handle non-finite values.
Results may differ from a plain program's by a relative error of at most 0.0065.
Values may be sent and summed in bfloat16 or wider, within the bound.
A program may use at most 192 MiB of HBM per device.

v0:
```python
import jax
import jax.numpy as jnp
from jax import lax
from jax.sharding import PartitionSpec as P

BLOCK_LEN = 256


def from_behind(shard, axis, by):
    peers = lax.axis_size(axis)
    pairs = [(i, i + by) for i in range(peers) if 0 <= i + by < peers]
    return lax.ppermute(shard, axis, pairs)


def causal_conv(padded, taps_weight, length):
    tap_count = taps_weight.shape[0]
    summed = jnp.zeros((length, taps_weight.shape[1]), jnp.float32)
    for tap_index in range(tap_count):
        summed = summed + taps_weight[tap_index] * padded[tap_index : tap_index + length].astype(
            jnp.float32
        )
    return jax.nn.silu(summed).astype(jnp.bfloat16)


def block_pass(carry, pieces):
    state_in, offset = carry
    inputs, b_rows, c_rows, step_rows, log_rows = pieces
    count = log_rows.shape[0]
    running = jnp.cumsum(log_rows, axis=0)
    scores = jnp.dot(c_rows, b_rows.T, preferred_element_type=jnp.float32)
    decay_gaps = running.T[:, :, None] - running.T[:, None, :]
    positions = jnp.arange(count)
    causal = positions[:, None] >= positions[None, :]
    decay_matrix = jnp.where(causal[None], jnp.exp(jnp.where(causal[None], decay_gaps, 0.0)), 0.0)
    weights = (scores[None] * decay_matrix * step_rows.T[:, None, :]).astype(jnp.bfloat16)
    inner_out = jnp.einsum("hts,shp->thp", weights, inputs, preferred_element_type=jnp.float32)
    block_total = running[-1]
    scaled = (
        (jnp.exp(block_total[None, :] - running) * step_rows)[:, :, None]
        * inputs.astype(jnp.float32)
    ).astype(jnp.bfloat16)
    block_state = jnp.einsum("shp,sn->hpn", scaled, b_rows, preferred_element_type=jnp.float32)
    carried = jnp.exp(running)[:, :, None] * jnp.einsum(
        "tn,hpn->thp", c_rows.astype(jnp.float32), state_in, precision=lax.Precision.HIGHEST
    )
    new_state = jnp.exp(block_total)[:, None, None] * state_in + block_state
    return ((new_state, offset + block_total), (inner_out + carried, running + offset[None, :]))


def per_device(x_raw, bc_raw, z_gate, conv_x, conv_bc, step_size, log_decay, skip_scale, norm_gain):
    tap_count = conv_x.shape[0]
    length, channels = x_raw.shape
    state_dim = bc_raw.shape[1] // 2
    head_count = step_size.shape[1]
    head_dim = channels // head_count
    tail_rows = jnp.concatenate(
        (x_raw[length - tap_count + 1 :], bc_raw[length - tap_count + 1 :]), axis=1
    )
    rim_rows = from_behind(tail_rows, "ctx", 1)
    x_conv = causal_conv(jnp.concatenate((rim_rows[:, :channels], x_raw), axis=0), conv_x, length)
    bc_conv = causal_conv(
        jnp.concatenate((rim_rows[:, channels:], bc_raw), axis=0), conv_bc, length
    )
    c_conv = bc_conv[:, state_dim:]
    blocks = length // BLOCK_LEN
    pieces = (
        x_conv.reshape(blocks, BLOCK_LEN, head_count, head_dim),
        bc_conv[:, :state_dim].reshape(blocks, BLOCK_LEN, state_dim),
        c_conv.reshape(blocks, BLOCK_LEN, state_dim),
        step_size.reshape(blocks, BLOCK_LEN, head_count),
        log_decay.reshape(blocks, BLOCK_LEN, head_count),
    )
    empty_state = jnp.zeros((head_count, head_dim, state_dim), jnp.float32)
    empty_total = jnp.zeros((head_count,), jnp.float32)
    (final_state, log_total), (local_out, running_dev) = lax.scan(
        block_pass, (empty_state, empty_total), pieces
    )
    local_out = local_out.reshape(length, head_count, head_dim)
    running_dev = running_dev.reshape(length, head_count)

    def relay_step(step_index, received):
        outgoing = jnp.exp(log_total)[:, None, None] * received + final_state
        return from_behind(outgoing, "ctx", 1)

    incoming = lax.fori_loop(0, lax.axis_size("ctx") - 1, relay_step, empty_state)
    correction = jnp.exp(running_dev)[:, :, None] * jnp.einsum(
        "tn,hpn->thp", c_conv.astype(jnp.float32), incoming, precision=lax.Precision.HIGHEST
    )
    ssm_out = (
        local_out
        + correction
        + skip_scale[None, :, None]
        * x_conv.reshape(length, head_count, head_dim).astype(jnp.float32)
    )
    gated_out = (
        ssm_out * jax.nn.silu(z_gate.astype(jnp.float32).reshape(length, head_count, head_dim))
    ).reshape(length, channels)
    partial_value = jnp.sum(gated_out * gated_out, axis=1)
    square_total = lax.psum(partial_value, "tp")
    mean_square = square_total / (channels * lax.axis_size("tp"))
    return (gated_out * lax.rsqrt(mean_square + 1e-05)[:, None] * norm_gain[None, :]).astype(
        jnp.bfloat16
    )


def solution(mesh):
    return jax.shard_map(
        per_device,
        mesh=mesh,
        in_specs=(
            P("ctx", "tp"),
            P("ctx", None),
            P("ctx", "tp"),
            P(None, "tp"),
            P(),
            P("ctx", "tp"),
            P("ctx", "tp"),
            P("tp"),
            P("tp"),
        ),
        out_specs=P("ctx", "tp"),
        check_vma=False,
    )
```

profile of v0, /device:TPU:16, one launch (start us, length us, event | category | flops | bytes accessed | tf_op | source)
XLA Modules:
  0.0 685.9 jit_solution(131324490015496725)
XLA Ops:
  12.4 10.8 %multiply_convert_fusion.6 = bf16[1536,1024]{1,0:T(8,128)(2,1)} fusion(bf16[1536,1024]{1,0:T(8,128)(2,1)} %param.13, bf16[3,1024]{1,0:T(4,128)(2,1)S(1)} %slice.94, f32[1024]{0:T(1024)S(1)} %bitcast.140, f32[1024]{0:T(1024)S(1)} %bitcast.141, f32[1024]{0:T(1024)S(1)} %bitcast.139, f32[1024]{0:T(1024)S(1)} %bitcast.138), kind=kLoop, calls=%fused_computation.56 | loop fusion | flops 39321600 | bytes 6313984 | tf_op jit(solution)/shard_map/convert_element_type | solution.py:22
  46.9 192.5 %while.30 = (s32[]{:T(128)}, f32[16,64,128]{2,1,0:T(8,128)S(1)}, f32[16]{0:T(128)S(1)}, f32[6,256,16,64]{1,0,3,2:T(8,128)}, f32[6,256,16]{1,2,0:T(8,128)}, /*ind...) while((s32[]{:T(128)}, f32[16,64,128]{2,1,0:T(8,128)S(1)}, ...), condition=%wide.region_3.4_spmd.clone, body=%wide.region_0.3_spmd.clone.sunk | while | flops 629493824 | bytes 11277725 | solution.py:75
  52.6 24.3 %dynamic_update_slice.14 = f32[6,256,16,64]{1,0,3,2:T(8,128)} dynamic-update-slice(f32[6,256,16,64]{1,0,3,2:T(8,128)} %get-tuple-element.337, f32[1,256,16,64]{1,0,3,2:T(1,128)S(1)} %copy.79, s32[]{:T(128)} %get-tuple-element.334, s32[]{:T(128)} %constant.46.clone.1..sunk, s32[]{:T(128)} %constant.46.clone.1..sunk, s32[]{:T(128)} %constant.46.clone.1..sunk) | dynamic-update-slice | bytes 2097156 | tf_op jit(solution)/shard_map/while/body/jit(dynamic_update_index_in_dim)/dynamic_update_slice | solution.py:75
  84.7 24.3 %dynamic_update_slice.14 = f32[6,256,16,64]{1,0,3,2:T(8,128)} dynamic-update-slice(f32[6,256,16,64]{1,0,3,2:T(8,128)} %get-tuple-element.337, f32[1,256,16,64]{1,0,3,2:T(1,128)S(1)} %copy.79, s32[]{:T(128)} %get-tuple-element.334, s32[]{:T(128)} %constant.46.clone.1..sunk, s32[]{:T(128)} %constant.46.clone.1..sunk, s32[]{:T(128)} %constant.46.clone.1..sunk) | dynamic-update-slice | bytes 2097156 | tf_op jit(solution)/shard_map/while/body/jit(dynamic_update_index_in_dim)/dynamic_update_slice | solution.py:75
  116.8 24.3 %dynamic_update_slice.14 = f32[6,256,16,64]{1,0,3,2:T(8,128)} dynamic-update-slice(f32[6,256,16,64]{1,0,3,2:T(8,128)} %get-tuple-element.337, f32[1,256,16,64]{1,0,3,2:T(1,128)S(1)} %copy.79, s32[]{:T(128)} %get-tuple-element.334, s32[]{:T(128)} %constant.46.clone.1..sunk, s32[]{:T(128)} %constant.46.clone.1..sunk, s32[]{:T(128)} %constant.46.clone.1..sunk) | dynamic-update-slice | bytes 2097156 | tf_op jit(solution)/shard_map/while/body/jit(dynamic_update_index_in_dim)/dynamic_update_slice | solution.py:75
  148.9 24.3 %dynamic_update_slice.14 = f32[6,256,16,64]{1,0,3,2:T(8,128)} dynamic-update-slice(f32[6,256,16,64]{1,0,3,2:T(8,128)} %get-tuple-element.337, f32[1,256,16,64]{1,0,3,2:T(1,128)S(1)} %copy.79, s32[]{:T(128)} %get-tuple-element.334, s32[]{:T(128)} %constant.46.clone.1..sunk, s32[]{:T(128)} %constant.46.clone.1..sunk, s32[]{:T(128)} %constant.46.clone.1..sunk) | dynamic-update-slice | bytes 2097156 | tf_op jit(solution)/shard_map/while/body/jit(dynamic_update_index_in_dim)/dynamic_update_slice | solution.py:75
  181.0 24.3 %dynamic_update_slice.14 = f32[6,256,16,64]{1,0,3,2:T(8,128)} dynamic-update-slice(f32[6,256,16,64]{1,0,3,2:T(8,128)} %get-tuple-element.337, f32[1,256,16,64]{1,0,3,2:T(1,128)S(1)} %copy.79, s32[]{:T(128)} %get-tuple-element.334, s32[]{:T(128)} %constant.46.clone.1..sunk, s32[]{:T(128)} %constant.46.clone.1..sunk, s32[]{:T(128)} %constant.46.clone.1..sunk) | dynamic-update-slice | bytes 2097156 | tf_op jit(solution)/shard_map/while/body/jit(dynamic_update_index_in_dim)/dynamic_update_slice | solution.py:75
  213.1 24.3 %dynamic_update_slice.14 = f32[6,256,16,64]{1,0,3,2:T(8,128)} dynamic-update-slice(f32[6,256,16,64]{1,0,3,2:T(8,128)} %get-tuple-element.337, f32[1,256,16,64]{1,0,3,2:T(1,128)S(1)} %copy.79, s32[]{:T(128)} %get-tuple-element.334, s32[]{:T(128)} %constant.46.clone.1..sunk, s32[]{:T(128)} %constant.46.clone.1..sunk, s32[]{:T(128)} %constant.46.clone.1..sunk) | dynamic-update-slice | bytes 2097156 | tf_op jit(solution)/shard_map/while/body/jit(dynamic_update_index_in_dim)/dynamic_update_slice | solution.py:75
  248.7 394.6 %while.29 = (s32[]{:T(128)}, f32[16,64,128]{2,1,0:T(8,128)S(1)}, f32[16,1,1]{0,2,1:T(1,128)S(1)}, f32[16,64,128]{2,1,0:T(8,128)S(1)}, s32[]{:T(128)}) while((s32[]{:T(128)}, f32[16,64,128]{2,1,0:T(8,128)S(1)}, f32[16,1,1]{0,2,1:T(1,128)S(1)}, f32[16,64,128]{2,1,0:T(8,128)S(1)}, s32[]{:T(128)}) %tuple.68), condition=%wide.region_5.6_spmd, body=%wide.region_4.5_spmd.sunk | while | flops 262146 | bytes 3670181 | solution.py:85
  263.5 10.7 %collective-permute-done = f32[16,64,128]{2,1,0:T(8,128)S(1)} collective-permute-done((f32[16,64,128]{2,1,0:T(8,128)S(1)}, f32[16,64,128]{2,1,0:T(8,128)S(1)}, u32[]{:S(2)}, u32[]{:S(2)}) %collective-permute-start) | collective-permute-done | bytes 524320 | tf_op jit(solution)/shard_map/while/body/eval_jaxpr/ppermute | solution.py:12
  276.2 10.7 %collective-permute-done = f32[16,64,128]{2,1,0:T(8,128)S(1)} collective-permute-done((f32[16,64,128]{2,1,0:T(8,128)S(1)}, f32[16,64,128]{2,1,0:T(8,128)S(1)}, u32[]{:S(2)}, u32[]{:S(2)}) %collective-permute-start) | collective-permute-done | bytes 524320 | tf_op jit(solution)/shard_map/while/body/eval_jaxpr/ppermute | solution.py:12
  289.0 10.7 %collective-permute-done = f32[16,64,128]{2,1,0:T(8,128)S(1)} collective-permute-done((f32[16,64,128]{2,1,0:T(8,128)S(1)}, f32[16,64,128]{2,1,0:T(8,128)S(1)}, u32[]{:S(2)}, u32[]{:S(2)}) %collective-permute-start) | collective-permute-done | bytes 524320 | tf_op jit(solution)/shard_map/while/body/eval_jaxpr/ppermute | solution.py:12
  301.7 10.7 %collective-permute-done = f32[16,64,128]{2,1,0:T(8,128)S(1)} collective-permute-done((f32[16,64,128]{2,1,0:T(8,128)S(1)}, f32[16,64,128]{2,1,0:T(8,128)S(1)}, u32[]{:S(2)}, u32[]{:S(2)}) %collective-permute-start) | collective-permute-done | bytes 524320 | tf_op jit(solution)/shard_map/while/body/eval_jaxpr/ppermute | solution.py:12
  314.4 10.7 %collective-permute-done = f32[16,64,128]{2,1,0:T(8,128)S(1)} collective-permute-done((f32[16,64,128]{2,1,0:T(8,128)S(1)}, f32[16,64,128]{2,1,0:T(8,128)S(1)}, u32[]{:S(2)}, u32[]{:S(2)}) %collective-permute-start) | collective-permute-done | bytes 524320 | tf_op jit(solution)/shard_map/while/body/eval_jaxpr/ppermute | solution.py:12
  327.2 10.7 %collective-permute-done = f32[16,64,128]{2,1,0:T(8,128)S(1)} collective-permute-done((f32[16,64,128]{2,1,0:T(8,128)S(1)}, f32[16,64,128]{2,1,0:T(8,128)S(1)}, u32[]{:S(2)}, u32[]{:S(2)}) %collective-permute-start) | collective-permute-done | bytes 524320 | tf_op jit(solution)/shard_map/while/body/eval_jaxpr/ppermute | solution.py:12
  339.9 10.7 %collective-permute-done = f32[16,64,128]{2,1,0:T(8,128)S(1)} collective-permute-done((f32[16,64,128]{2,1,0:T(8,128)S(1)}, f32[16,64,128]{2,1,0:T(8,128)S(1)}, u32[]{:S(2)}, u32[]{:S(2)}) %collective-permute-start) | collective-permute-done | bytes 524320 | tf_op jit(solution)/shard_map/while/body/eval_jaxpr/ppermute | solution.py:12
  352.6 10.7 %collective-permute-done = f32[16,64,128]{2,1,0:T(8,128)S(1)} collective-permute-done((f32[16,64,128]{2,1,0:T(8,128)S(1)}, f32[16,64,128]{2,1,0:T(8,128)S(1)}, u32[]{:S(2)}, u32[]{:S(2)}) %collective-permute-start) | collective-permute-done | bytes 524320 | tf_op jit(solution)/shard_map/while/body/eval_jaxpr/ppermute | solution.py:12
  365.4 10.7 %collective-permute-done = f32[16,64,128]{2,1,0:T(8,128)S(1)} collective-permute-done((f32[16,64,128]{2,1,0:T(8,128)S(1)}, f32[16,64,128]{2,1,0:T(8,128)S(1)}, u32[]{:S(2)}, u32[]{:S(2)}) %collective-permute-start) | collective-permute-done | bytes 524320 | tf_op jit(solution)/shard_map/while/body/eval_jaxpr/ppermute | solution.py:12
  378.1 10.7 %collective-permute-done = f32[16,64,128]{2,1,0:T(8,128)S(1)} collective-permute-done((f32[16,64,128]{2,1,0:T(8,128)S(1)}, f32[16,64,128]{2,1,0:T(8,128)S(1)}, u32[]{:S(2)}, u32[]{:S(2)}) %collective-permute-start) | collective-permute-done | bytes 524320 | tf_op jit(solution)/shard_map/while/body/eval_jaxpr/ppermute | solution.py:12
  390.8 10.7 %collective-permute-done = f32[16,64,128]{2,1,0:T(8,128)S(1)} collective-permute-done((f32[16,64,128]{2,1,0:T(8,128)S(1)}, f32[16,64,128]{2,1,0:T(8,128)S(1)}, u32[]{:S(2)}, u32[]{:S(2)}) %collective-permute-start) | collective-permute-done | bytes 524320 | tf_op jit(solution)/shard_map/while/body/eval_jaxpr/ppermute | solution.py:12
  403.5 10.7 %collective-permute-done = f32[16,64,128]{2,1,0:T(8,128)S(1)} collective-permute-done((f32[16,64,128]{2,1,0:T(8,128)S(1)}, f32[16,64,128]{2,1,0:T(8,128)S(1)}, u32[]{:S(2)}, u32[]{:S(2)}) %collective-permute-start) | collective-permute-done | bytes 524320 | tf_op jit(solution)/shard_map/while/body/eval_jaxpr/ppermute | solution.py:12
  416.3 10.7 %collective-permute-done = f32[16,64,128]{2,1,0:T(8,128)S(1)} collective-permute-done((f32[16,64,128]{2,1,0:T(8,128)S(1)}, f32[16,64,128]{2,1,0:T(8,128)S(1)}, u32[]{:S(2)}, u32[]{:S(2)}) %collective-permute-start) | collective-permute-done | bytes 524320 | tf_op jit(solution)/shard_map/while/body/eval_jaxpr/ppermute | solution.py:12
  429.0 10.7 %collective-permute-done = f32[16,64,128]{2,1,0:T(8,128)S(1)} collective-permute-done((f32[16,64,128]{2,1,0:T(8,128)S(1)}, f32[16,64,128]{2,1,0:T(8,128)S(1)}, u32[]{:S(2)}, u32[]{:S(2)}) %collective-permute-start) | collective-permute-done | bytes 524320 | tf_op jit(solution)/shard_map/while/body/eval_jaxpr/ppermute | solution.py:12
  660.6 20.2 %psum.7 = f32[1536]{0:T(1024)S(1)} all-reduce(f32[1536]{0:T(1024)S(1)} %get-tuple-element.215), channel_id=1, replica_groups=mesh['ctx'=32,'tp'=8] {'tp'}, use_global_device_ids=true, to_apply=%region_7.8 | all-reduce | flops 1536 | bytes 12288 | tf_op jit(solution)/shard_map/psum | solution.py:99
  (225 shorter events, 358.6 us)
Async XLA Ops:
  248.8 12.6 %collective-permute-start = (f32[16,64,128]{2,1,0:T(8,128)S(1)}, f32[16,64,128]{2,1,0:T(8,128)S(1)}, u32[]{:S(2)}, u32[]{:S(2)}) collective-permute-start(f32[16,64,128]{2,1,0:T(8,128)S(1)} %multiply_add_fusion.2), channel_id=1, source_target_pairs={{0,8},{8,16},{16,24},{24,32},{32,40},{40,48},{48,56},{56,64},{64,7... | collective-permute-start | bytes 1572872 | tf_op jit(solution)/shard_map/while/body/eval_jaxpr/ppermute | solution.py:12
  261.6 12.6 %collective-permute-start = (f32[16,64,128]{2,1,0:T(8,128)S(1)}, f32[16,64,128]{2,1,0:T(8,128)S(1)}, u32[]{:S(2)}, u32[]{:S(2)}) collective-permute-start(f32[16,64,128]{2,1,0:T(8,128)S(1)} %multiply_add_fusion.2), channel_id=1, source_target_pairs={{0,8},{8,16},{16,24},{24,32},{32,40},{40,48},{48,56},{56,64},{64,7... | collective-permute-start | bytes 1572872 | tf_op jit(solution)/shard_map/while/body/eval_jaxpr/ppermute | solution.py:12
  274.3 12.6 %collective-permute-start = (f32[16,64,128]{2,1,0:T(8,128)S(1)}, f32[16,64,128]{2,1,0:T(8,128)S(1)}, u32[]{:S(2)}, u32[]{:S(2)}) collective-permute-start(f32[16,64,128]{2,1,0:T(8,128)S(1)} %multiply_add_fusion.2), channel_id=1, source_target_pairs={{0,8},{8,16},{16,24},{24,32},{32,40},{40,48},{48,56},{56,64},{64,7... | collective-permute-start | bytes 1572872 | tf_op jit(solution)/shard_map/while/body/eval_jaxpr/ppermute | solution.py:12
  287.0 12.6 %collective-permute-start = (f32[16,64,128]{2,1,0:T(8,128)S(1)}, f32[16,64,128]{2,1,0:T(8,128)S(1)}, u32[]{:S(2)}, u32[]{:S(2)}) collective-permute-start(f32[16,64,128]{2,1,0:T(8,128)S(1)} %multiply_add_fusion.2), channel_id=1, source_target_pairs={{0,8},{8,16},{16,24},{24,32},{32,40},{40,48},{48,56},{56,64},{64,7... | collective-permute-start | bytes 1572872 | tf_op jit(solution)/shard_map/while/body/eval_jaxpr/ppermute | solution.py:12
  299.8 12.6 %collective-permute-start = (f32[16,64,128]{2,1,0:T(8,128)S(1)}, f32[16,64,128]{2,1,0:T(8,128)S(1)}, u32[]{:S(2)}, u32[]{:S(2)}) collective-permute-start(f32[16,64,128]{2,1,0:T(8,128)S(1)} %multiply_add_fusion.2), channel_id=1, source_target_pairs={{0,8},{8,16},{16,24},{24,32},{32,40},{40,48},{48,56},{56,64},{64,7... | collective-permute-start | bytes 1572872 | tf_op jit(solution)/shard_map/while/body/eval_jaxpr/ppermute | solution.py:12
  312.5 12.6 %collective-permute-start = (f32[16,64,128]{2,1,0:T(8,128)S(1)}, f32[16,64,128]{2,1,0:T(8,128)S(1)}, u32[]{:S(2)}, u32[]{:S(2)}) collective-permute-start(f32[16,64,128]{2,1,0:T(8,128)S(1)} %multiply_add_fusion.2), channel_id=1, source_target_pairs={{0,8},{8,16},{16,24},{24,32},{32,40},{40,48},{48,56},{56,64},{64,7... | collective-permute-start | bytes 1572872 | tf_op jit(solution)/shard_map/while/body/eval_jaxpr/ppermute | solution.py:12
  325.2 12.6 %collective-permute-start = (f32[16,64,128]{2,1,0:T(8,128)S(1)}, f32[16,64,128]{2,1,0:T(8,128)S(1)}, u32[]{:S(2)}, u32[]{:S(2)}) collective-permute-start(f32[16,64,128]{2,1,0:T(8,128)S(1)} %multiply_add_fusion.2), channel_id=1, source_target_pairs={{0,8},{8,16},{16,24},{24,32},{32,40},{40,48},{48,56},{56,64},{64,7... | collective-permute-start | bytes 1572872 | tf_op jit(solution)/shard_map/while/body/eval_jaxpr/ppermute | solution.py:12
  338.0 12.6 %collective-permute-start = (f32[16,64,128]{2,1,0:T(8,128)S(1)}, f32[16,64,128]{2,1,0:T(8,128)S(1)}, u32[]{:S(2)}, u32[]{:S(2)}) collective-permute-start(f32[16,64,128]{2,1,0:T(8,128)S(1)} %multiply_add_fusion.2), channel_id=1, source_target_pairs={{0,8},{8,16},{16,24},{24,32},{32,40},{40,48},{48,56},{56,64},{64,7... | collective-permute-start | bytes 1572872 | tf_op jit(solution)/shard_map/while/body/eval_jaxpr/ppermute | solution.py:12
  350.7 12.6 %collective-permute-start = (f32[16,64,128]{2,1,0:T(8,128)S(1)}, f32[16,64,128]{2,1,0:T(8,128)S(1)}, u32[]{:S(2)}, u32[]{:S(2)}) collective-permute-start(f32[16,64,128]{2,1,0:T(8,128)S(1)} %multiply_add_fusion.2), channel_id=1, source_target_pairs={{0,8},{8,16},{16,24},{24,32},{32,40},{40,48},{48,56},{56,64},{64,7... | collective-permute-start | bytes 1572872 | tf_op jit(solution)/shard_map/while/body/eval_jaxpr/ppermute | solution.py:12
  363.4 12.6 %collective-permute-start = (f32[16,64,128]{2,1,0:T(8,128)S(1)}, f32[16,64,128]{2,1,0:T(8,128)S(1)}, u32[]{:S(2)}, u32[]{:S(2)}) collective-permute-start(f32[16,64,128]{2,1,0:T(8,128)S(1)} %multiply_add_fusion.2), channel_id=1, source_target_pairs={{0,8},{8,16},{16,24},{24,32},{32,40},{40,48},{48,56},{56,64},{64,7... | collective-permute-start | bytes 1572872 | tf_op jit(solution)/shard_map/while/body/eval_jaxpr/ppermute | solution.py:12
  376.1 12.6 %collective-permute-start = (f32[16,64,128]{2,1,0:T(8,128)S(1)}, f32[16,64,128]{2,1,0:T(8,128)S(1)}, u32[]{:S(2)}, u32[]{:S(2)}) collective-permute-start(f32[16,64,128]{2,1,0:T(8,128)S(1)} %multiply_add_fusion.2), channel_id=1, source_target_pairs={{0,8},{8,16},{16,24},{24,32},{32,40},{40,48},{48,56},{56,64},{64,7... | collective-permute-start | bytes 1572872 | tf_op jit(solution)/shard_map/while/body/eval_jaxpr/ppermute | solution.py:12
  388.9 12.6 %collective-permute-start = (f32[16,64,128]{2,1,0:T(8,128)S(1)}, f32[16,64,128]{2,1,0:T(8,128)S(1)}, u32[]{:S(2)}, u32[]{:S(2)}) collective-permute-start(f32[16,64,128]{2,1,0:T(8,128)S(1)} %multiply_add_fusion.2), channel_id=1, source_target_pairs={{0,8},{8,16},{16,24},{24,32},{32,40},{40,48},{48,56},{56,64},{64,7... | collective-permute-start | bytes 1572872 | tf_op jit(solution)/shard_map/while/body/eval_jaxpr/ppermute | solution.py:12
  401.6 12.6 %collective-permute-start = (f32[16,64,128]{2,1,0:T(8,128)S(1)}, f32[16,64,128]{2,1,0:T(8,128)S(1)}, u32[]{:S(2)}, u32[]{:S(2)}) collective-permute-start(f32[16,64,128]{2,1,0:T(8,128)S(1)} %multiply_add_fusion.2), channel_id=1, source_target_pairs={{0,8},{8,16},{16,24},{24,32},{32,40},{40,48},{48,56},{56,64},{64,7... | collective-permute-start | bytes 1572872 | tf_op jit(solution)/shard_map/while/body/eval_jaxpr/ppermute | solution.py:12
  414.3 12.6 %collective-permute-start = (f32[16,64,128]{2,1,0:T(8,128)S(1)}, f32[16,64,128]{2,1,0:T(8,128)S(1)}, u32[]{:S(2)}, u32[]{:S(2)}) collective-permute-start(f32[16,64,128]{2,1,0:T(8,128)S(1)} %multiply_add_fusion.2), channel_id=1, source_target_pairs={{0,8},{8,16},{16,24},{24,32},{32,40},{40,48},{48,56},{56,64},{64,7... | collective-permute-start | bytes 1572872 | tf_op jit(solution)/shard_map/while/body/eval_jaxpr/ppermute | solution.py:12
  427.1 12.6 %collective-permute-start = (f32[16,64,128]{2,1,0:T(8,128)S(1)}, f32[16,64,128]{2,1,0:T(8,128)S(1)}, u32[]{:S(2)}, u32[]{:S(2)}) collective-permute-start(f32[16,64,128]{2,1,0:T(8,128)S(1)} %multiply_add_fusion.2), channel_id=1, source_target_pairs={{0,8},{8,16},{16,24},{24,32},{32,40},{40,48},{48,56},{56,64},{64,7... | collective-permute-start | bytes 1572872 | tf_op jit(solution)/shard_map/while/body/eval_jaxpr/ppermute | solution.py:12
  439.8 12.6 %collective-permute-start = (f32[16,64,128]{2,1,0:T(8,128)S(1)}, f32[16,64,128]{2,1,0:T(8,128)S(1)}, u32[]{:S(2)}, u32[]{:S(2)}) collective-permute-start(f32[16,64,128]{2,1,0:T(8,128)S(1)} %multiply_add_fusion.2), channel_id=1, source_target_pairs={{0,8},{8,16},{16,24},{24,32},{32,40},{40,48},{48,56},{56,64},{64,7... | collective-permute-start | bytes 1572872 | tf_op jit(solution)/shard_map/while/body/eval_jaxpr/ppermute | solution.py:12
  452.5 12.6 %collective-permute-start = (f32[16,64,128]{2,1,0:T(8,128)S(1)}, f32[16,64,128]{2,1,0:T(8,128)S(1)}, u32[]{:S(2)}, u32[]{:S(2)}) collective-permute-start(f32[16,64,128]{2,1,0:T(8,128)S(1)} %multiply_add_fusion.2), channel_id=1, source_target_pairs={{0,8},{8,16},{16,24},{24,32},{32,40},{40,48},{48,56},{56,64},{64,7... | collective-permute-start | bytes 1572872 | tf_op jit(solution)/shard_map/while/body/eval_jaxpr/ppermute | solution.py:12
  465.3 12.6 %collective-permute-start = (f32[16,64,128]{2,1,0:T(8,128)S(1)}, f32[16,64,128]{2,1,0:T(8,128)S(1)}, u32[]{:S(2)}, u32[]{:S(2)}) collective-permute-start(f32[16,64,128]{2,1,0:T(8,128)S(1)} %multiply_add_fusion.2), channel_id=1, source_target_pairs={{0,8},{8,16},{16,24},{24,32},{32,40},{40,48},{48,56},{56,64},{64,7... | collective-permute-start | bytes 1572872 | tf_op jit(solution)/shard_map/while/body/eval_jaxpr/ppermute | solution.py:12
  478.0 12.6 %collective-permute-start = (f32[16,64,128]{2,1,0:T(8,128)S(1)}, f32[16,64,128]{2,1,0:T(8,128)S(1)}, u32[]{:S(2)}, u32[]{:S(2)}) collective-permute-start(f32[16,64,128]{2,1,0:T(8,128)S(1)} %multiply_add_fusion.2), channel_id=1, source_target_pairs={{0,8},{8,16},{16,24},{24,32},{32,40},{40,48},{48,56},{56,64},{64,7... | collective-permute-start | bytes 1572872 | tf_op jit(solution)/shard_map/while/body/eval_jaxpr/ppermute | solution.py:12
  490.7 12.6 %collective-permute-start = (f32[16,64,128]{2,1,0:T(8,128)S(1)}, f32[16,64,128]{2,1,0:T(8,128)S(1)}, u32[]{:S(2)}, u32[]{:S(2)}) collective-permute-start(f32[16,64,128]{2,1,0:T(8,128)S(1)} %multiply_add_fusion.2), channel_id=1, source_target_pairs={{0,8},{8,16},{16,24},{24,32},{32,40},{40,48},{48,56},{56,64},{64,7... | collective-permute-start | bytes 1572872 | tf_op jit(solution)/shard_map/while/body/eval_jaxpr/ppermute | solution.py:12
  503.4 12.6 %collective-permute-start = (f32[16,64,128]{2,1,0:T(8,128)S(1)}, f32[16,64,128]{2,1,0:T(8,128)S(1)}, u32[]{:S(2)}, u32[]{:S(2)}) collective-permute-start(f32[16,64,128]{2,1,0:T(8,128)S(1)} %multiply_add_fusion.2), channel_id=1, source_target_pairs={{0,8},{8,16},{16,24},{24,32},{32,40},{40,48},{48,56},{56,64},{64,7... | collective-permute-start | bytes 1572872 | tf_op jit(solution)/shard_map/while/body/eval_jaxpr/ppermute | solution.py:12
  516.2 12.6 %collective-permute-start = (f32[16,64,128]{2,1,0:T(8,128)S(1)}, f32[16,64,128]{2,1,0:T(8,128)S(1)}, u32[]{:S(2)}, u32[]{:S(2)}) collective-permute-start(f32[16,64,128]{2,1,0:T(8,128)S(1)} %multiply_add_fusion.2), channel_id=1, source_target_pairs={{0,8},{8,16},{16,24},{24,32},{32,40},{40,48},{48,56},{56,64},{64,7... | collective-permute-start | bytes 1572872 | tf_op jit(solution)/shard_map/while/body/eval_jaxpr/ppermute | solution.py:12
  528.9 12.6 %collective-permute-start = (f32[16,64,128]{2,1,0:T(8,128)S(1)}, f32[16,64,128]{2,1,0:T(8,128)S(1)}, u32[]{:S(2)}, u32[]{:S(2)}) collective-permute-start(f32[16,64,128]{2,1,0:T(8,128)S(1)} %multiply_add_fusion.2), channel_id=1, source_target_pairs={{0,8},{8,16},{16,24},{24,32},{32,40},{40,48},{48,56},{56,64},{64,7... | collective-permute-start | bytes 1572872 | tf_op jit(solution)/shard_map/while/body/eval_jaxpr/ppermute | solution.py:12
  541.6 12.6 %collective-permute-start = (f32[16,64,128]{2,1,0:T(8,128)S(1)}, f32[16,64,128]{2,1,0:T(8,128)S(1)}, u32[]{:S(2)}, u32[]{:S(2)}) collective-permute-start(f32[16,64,128]{2,1,0:T(8,128)S(1)} %multiply_add_fusion.2), channel_id=1, source_target_pairs={{0,8},{8,16},{16,24},{24,32},{32,40},{40,48},{48,56},{56,64},{64,7... | collective-permute-start | bytes 1572872 | tf_op jit(solution)/shard_map/while/body/eval_jaxpr/ppermute | solution.py:12
  (12 other events, 535.6 us)
where the time goes:
time: 692 us; the launch traced here: 686 us
  waiting for transfers between devices  329 us (48%)
  local copies, waits for them, and re-layouts  203 us (29%)
  starting transfers between devices  63 us (9%)
  matrix products  39.1 us (6%)
  other arithmetic  29.3 us (4%)
  blocking collectives  20.2 us (3%)
    ppermute x32, waiting for transfers between devices, from_behind(): return lax.ppermute(shard, axis, pairs)  329 us
    dynamic_update_slice x12, local copies, waits for them, and re-layouts, per_device(): lax.scan(block_pass, (empty_state, empty_total), pieces)  152 us
    ppermute x32, starting transfers between devices, from_behind(): return lax.ppermute(shard, axis, pairs)  63 us
    psum x1, blocking collectives, per_device(): square_total = lax.psum(partial_value, 'tp')  20.2 us
    dot_general x6, matrix products, block_pass(): jnp.einsum('hts,shp->thp', weights, inputs, preferred_element_type=jnp.fl...  15.6 us
  transfers between devices with their start and end apart: 32, of which 31 were waited for; matrix products, arithmetic and copies ran while one was open for 1% of the time, Pallas kernels for 0%

commit v1 on v0

v1 whole, which is shorter than its diff:
```python
import functools

import jax
import jax.numpy as jnp
from jax import lax
from jax.experimental import pallas as pl
from jax.experimental.pallas import tpu as pltpu
from jax.sharding import PartitionSpec as P

F32 = jnp.float32
BF16 = jnp.bfloat16
MESH = pl.DeviceIdType.MESH
CHUNK = 128
GROUP = 256
HALO = 16


def split2(value):
    high = value.astype(BF16)
    return high, (value - high.astype(F32)).astype(BF16)


def split3(value):
    high = value.astype(BF16)
    rest = value - high.astype(F32)
    mid = rest.astype(BF16)
    return high, mid, (rest - mid.astype(F32)).astype(BF16)


def silu(value):
    half = 0.5 * value
    return half * jnp.tanh(half) + half


def conv_silu(rows, taps):
    wide = rows.astype(F32)[8:]
    behind = pltpu.roll(wide, 1, 0)
    near = taps[3] * wide + taps[2] * behind
    far = taps[1] * wide + taps[0] * behind
    return silu((near + pltpu.roll(far, 2, 0))[8:])


def mixer(
    ctx_size, tp_size, head_dim,
    x_hbm, bc_hbm, z_hbm, convx_ref, convbc_ref, step_hbm, log_hbm, skip_ref,
    g_hbm, ssq_ref,
    xbuf, bcbuf, zbuf, stepbuf, logbuf, spread, tri, fin, fout, rowbuf, rows_ref,
    sc, bt, xconv, xs, state, parts, recv, lam_own, lam, lam_wide, send, start_state,
    local_ref, gate_ref, gbuf, ssq, ssq_recv,
    load_sem, halo_send, halo_recv, lam_send, lam_recv, part_send, part_recv,
    start_send, start_recv, ssq_send, ssq_recv_sem, out_sem,
):
    length, channels = x_hbm.shape
    heads = step_hbm.shape[1]
    chunks = length // CHUNK
    groups = channels // GROUP
    n_state = bt.shape[1]
    part_rows = parts.shape[1]
    per_group = ctx_size // groups
    mid = CHUNK // 2 - 1
    me = lax.axis_index("ctx")
    tp = lax.axis_index("tp")

    def cols(g):
        return slice(g * GROUP, (g + 1) * GROUP)

    loads = [
        pltpu.make_async_copy(log_hbm, logbuf, load_sem.at[0]),
        pltpu.make_async_copy(step_hbm, stepbuf, load_sem.at[1]),
        pltpu.make_async_copy(bc_hbm, bcbuf.at[pl.ds(HALO, length)], load_sem.at[2]),
    ]
    x_loads = [
        pltpu.make_async_copy(
            x_hbm.at[:, cols(g)], xbuf.at[pl.ds(HALO, length), cols(g)], load_sem.at[4 + g]
        )
        for g in range(groups)
    ]
    z_load = pltpu.make_async_copy(z_hbm, zbuf, load_sem.at[3])
    for load in loads + x_loads + [z_load]:
        load.start()

    barrier = pltpu.get_barrier_semaphore()

    def greet_ctx(k, _):
        pl.semaphore_signal(barrier, inc=1, device_id=(lax.rem(me + k, ctx_size), tp), device_id_type=MESH)
        return 0

    def greet_tp(k, _):
        pl.semaphore_signal(barrier, inc=1, device_id=(me, lax.rem(tp + k, tp_size)), device_id_type=MESH)
        return 0

    lax.fori_loop(1, ctx_size, greet_ctx, 0)
    lax.fori_loop(1, tp_size, greet_tp, 0)

    t_at = lax.broadcasted_iota(jnp.int32, (CHUNK, CHUNK), 0)
    s_at = lax.broadcasted_iota(jnp.int32, (CHUNK, CHUNK), 1)
    lower = jnp.where(t_at >= s_at, 1.0, 0.0).astype(BF16)
    for k in range(3):
        tri[:, k * CHUNK : (k + 1) * CHUNK] = lower
    head_at = lax.broadcasted_iota(jnp.int32, (heads, channels), 0)
    channel_at = lax.broadcasted_iota(jnp.int32, (heads, channels), 1)
    first = head_at * head_dim
    one_map = jnp.where((channel_at >= first) & (channel_at < first + head_dim), 1.0, 0.0).astype(BF16)
    for k in range(3):
        spread[k * heads : (k + 1) * heads, :] = one_map
    rowbuf[...] = jnp.zeros_like(rowbuf)

    loads[0].wait()
    loads[1].wait()
    low_lane = lax.broadcasted_iota(jnp.int32, (CHUNK, 2 * heads), 1) < heads

    def two_halves(value):
        high = value.astype(BF16).astype(F32)
        return jnp.where(low_lane, high, value - high).astype(BF16)

    def decays(c, carry):
        before, tail = carry
        at = pl.multiple_of(c * CHUNK, CHUNK)
        pieces = jnp.concatenate(split3(logbuf[pl.ds(at, CHUNK), :]), axis=0)
        running = jnp.dot(tri[...], pieces, preferred_element_type=F32)
        middle = running[mid : mid + 1]
        end = running[CHUNK - 1 : CHUNK]
        centred = running - middle
        centred = jnp.concatenate((centred, centred), axis=1)
        steps = stepbuf[pl.ds(at, CHUNK), :]
        steps = jnp.concatenate((steps, steps), axis=1)
        fin[pl.ds(at, CHUNK), :] = two_halves(jnp.exp(-centred) * steps)
        fout[pl.ds(at, CHUNK), :] = two_halves(jnp.exp(centred))
        rowbuf[pl.ds(c, 1), :] = jnp.exp(middle + tail)
        rowbuf[pl.ds(16 + c, 1), :] = jnp.exp(before + middle)
        return before + end, end - middle

    zero_row = jnp.zeros((1, heads), F32)
    total, tail = lax.fori_loop(0, chunks, decays, (zero_row, zero_row))
    rowbuf[chunks : chunks + 1, :] = jnp.exp(tail)
    rowbuf[30:31, :] = skip_ref[...]
    rows_ref[...] = jnp.dot(
        jnp.concatenate(split3(rowbuf[...]), axis=1), spread[...], preferred_element_type=F32
    )
    lam_own[...] = jnp.zeros_like(lam_own)
    lam_own[0:1, 0:heads] = jnp.exp(total)
    lam[me] = lam_own[...]

    pl.semaphore_wait(barrier, ctx_size + tp_size - 2)

    right = lax.rem(me + 1, ctx_size)
    x_halo = pltpu.make_async_remote_copy(
        src_ref=x_hbm.at[pl.ds(length - HALO, HALO)], dst_ref=xbuf.at[pl.ds(0, HALO)],
        send_sem=halo_send.at[0], recv_sem=halo_recv.at[0], device_id=(right, tp), device_id_type=MESH,
    )
    bc_halo = pltpu.make_async_remote_copy(
        src_ref=bc_hbm.at[pl.ds(length - HALO, HALO)], dst_ref=bcbuf.at[pl.ds(0, HALO)],
        send_sem=halo_send.at[1], recv_sem=halo_recv.at[1], device_id=(right, tp), device_id_type=MESH,
    )
    bc_halo.start()
    x_halo.start()

    def lam_copy(dst, src):
        return pltpu.make_async_remote_copy(
            src_ref=lam_own, dst_ref=lam.at[src], send_sem=lam_send.at[dst], recv_sem=lam_recv.at[src],
            device_id=(dst, tp), device_id_type=MESH,
        )

    def part_copy(dst, src):
        return pltpu.make_async_remote_copy(
            src_ref=parts.at[dst], dst_ref=recv.at[src], send_sem=part_send.at[dst],
            recv_sem=part_recv.at[src], device_id=(dst, tp), device_id_type=MESH,
        )

    def start_copy(dst, src):
        row = pl.multiple_of((src // groups) * part_rows, part_rows)
        return pltpu.make_async_remote_copy(
            src_ref=send.at[dst], dst_ref=start_state.at[lax.rem(src, groups), pl.ds(row, part_rows)],
            send_sem=start_send.at[dst], recv_sem=start_recv.at[src], device_id=(dst, tp), device_id_type=MESH,
        )

    def ssq_copy(dst, src):
        return pltpu.make_async_remote_copy(
            src_ref=ssq, dst_ref=ssq_recv.at[src], send_sem=ssq_send.at[dst],
            recv_sem=ssq_recv_sem.at[src], device_id=(me, dst), device_id_type=MESH,
        )

    def each_peer(fn):
        def step(k, _):
            fn(lax.rem(me + k, ctx_size))
            return 0

        lax.fori_loop(1, ctx_size, step, 0)

    def each_tp(fn):
        def step(k, _):
            fn(lax.rem(tp + k, tp_size))
            return 0

        lax.fori_loop(1, tp_size, step, 0)

    each_peer(lambda d: lam_copy(d, me).start())

    loads[2].wait()
    bc_taps = [convbc_ref[k : k + 1, :] for k in range(4)]

    def project(c):
        at = pl.multiple_of(c * CHUNK, CHUNK)
        both = conv_silu(bcbuf[pl.ds(at, CHUNK + HALO), :], bc_taps).astype(BF16)
        c_rows = both[:, n_state:]
        b_turned = both[:, :n_state].T
        bt[c] = b_turned
        scores = jnp.dot(c_rows, b_turned, preferred_element_type=F32)
        causal = lax.broadcasted_iota(jnp.int32, (CHUNK, CHUNK), 0) >= lax.broadcasted_iota(
            jnp.int32, (CHUNK, CHUNK), 1
        )
        sc[c, :, :CHUNK] = jnp.where(causal, scores, 0.0).astype(BF16)
        sc[c, :, CHUNK:] = c_rows

    def project_step(c, _):
        project(c)
        return 0

    lax.fori_loop(1, chunks, project_step, 0)
    bc_halo.wait_recv()
    x_halo.wait_recv()
    bcbuf[0:HALO, :] = jnp.where(me > 0, bcbuf[0:HALO, :].astype(F32), 0.0).astype(BF16)
    xbuf[0:HALO, :] = jnp.where(me > 0, xbuf[0:HALO, :].astype(F32), 0.0).astype(BF16)
    project(0)

    def carry_through():
        each_peer(lambda s: lam_copy(s, s).wait_recv())
        each_peer(lambda s: part_copy(s, s).wait_recv())
        col = pl.multiple_of(lax.rem(me, groups) * GROUP, GROUP)
        lam_wide[...] = jnp.dot(
            jnp.concatenate(split3(lam[:, 0, :heads]), axis=1), spread[:, pl.ds(col, GROUP)],
            preferred_element_type=F32,
        )

        def step(d, running):
            send[d] = running.astype(BF16)
            return lam_wide[pl.ds(d, 1), :] * running + recv[d].astype(F32)

        lax.fori_loop(0, ctx_size, step, jnp.zeros((part_rows, GROUP), F32), unroll=4)
        row = pl.multiple_of((me // groups) * part_rows, part_rows)
        start_state[lax.rem(me, groups), pl.ds(row, part_rows), :] = send[me]
        each_peer(lambda d: start_copy(d, me).start())

    for g in range(groups):
        x_loads[g].wait()
        taps = [convx_ref[k : k + 1, cols(g)] for k in range(4)]
        state[...] = jnp.zeros_like(state)

        def forward(c, _, g=g, taps=taps):
            at = pl.multiple_of(c * CHUNK, CHUNK)
            value = conv_silu(xbuf[pl.ds(at, CHUNK + HALO), cols(g)], taps)
            xconv[pl.ds(at, CHUNK), cols(g)] = value.astype(BF16)
            scale = jnp.dot(fin[pl.ds(at, CHUNK), :], spread[: 2 * heads, cols(g)], preferred_element_type=F32)
            scaled = (value * scale).astype(BF16)
            held = state[...]
            xs[c, :CHUNK, cols(g)] = scaled
            xs[c, CHUNK:, cols(g)] = held.astype(BF16)
            added = jnp.dot(bt[c], scaled, preferred_element_type=F32)
            state[...] = rows_ref[pl.ds(c + 1, 1), cols(g)] * (held + added)
            return 0

        lax.fori_loop(0, chunks, forward, 0)
        for r in range(per_group):
            parts[r * groups + g] = state[r * part_rows : (r + 1) * part_rows, :].astype(BF16)

        @pl.when(lax.rem(me, groups) == g)
        def _():
            recv[me] = parts[me]

        def send_part(k, _, g=g):
            dst = lax.rem(me // groups + k, per_group) * groups + g

            @pl.when(dst != me)
            def _():
                part_copy(dst, me).start()

            return 0

        lax.fori_loop(0, per_group, send_part, 0)
        if g > 0:
            pl.when(lax.rem(me, groups) == g - 1)(carry_through)

    z_load.wait()

    def local(c, _):
        at = pl.multiple_of(c * CHUNK, CHUNK)
        for g in range(groups):
            inner = jnp.dot(sc[c], xs[c, :, cols(g)], preferred_element_type=F32)
            scale = jnp.dot(fout[pl.ds(at, CHUNK), :], spread[: 2 * heads, cols(g)], preferred_element_type=F32)
            gate = silu(zbuf[pl.ds(at, CHUNK), cols(g)].astype(F32))
            skipped = rows_ref[30:31, cols(g)] * xconv[pl.ds(at, CHUNK), cols(g)].astype(F32)
            local_ref[pl.ds(at, CHUNK), cols(g)] = (inner * scale + skipped) * gate
            gate_ref[pl.ds(at, CHUNK), cols(g)] = (
                scale * gate * rows_ref[pl.ds(16 + c, 1), cols(g)]
            ).astype(BF16)
        return 0

    lax.fori_loop(0, chunks // 2, local, 0)
    pl.when(lax.rem(me, groups) == groups - 1)(carry_through)
    lax.fori_loop(chunks // 2, chunks, local, 0)

    each_peer(lambda s: start_copy(s, s).wait_recv())
    ssq[...] = jnp.zeros_like(ssq)

    def out_copy(c):
        at = pl.multiple_of(c * CHUNK, CHUNK)
        return pltpu.make_async_copy(gbuf.at[pl.ds(at, CHUNK)], g_hbm.at[pl.ds(at, CHUNK)], out_sem.at[c])

    def finish(c, _):
        at = pl.multiple_of(c * CHUNK, CHUNK)
        squares = jnp.zeros((CHUNK, 128), F32)
        for g in range(groups):
            carried = jnp.dot(sc[c, :, CHUNK:], start_state[g], preferred_element_type=F32)
            gated = local_ref[pl.ds(at, CHUNK), cols(g)] + gate_ref[pl.ds(at, CHUNK), cols(g)].astype(F32) * carried
            gbuf[pl.ds(at, CHUNK), cols(g)] = gated.astype(BF16)
            both = gated * gated
            for lane in range(0, GROUP, 128):
                squares = squares + both[:, lane : lane + 128]
        ssq[pl.ds(c, 1), :] = jnp.sum(squares.T, axis=0, keepdims=True)
        out_copy(c).start()
        return 0

    lax.fori_loop(0, chunks, finish, 0)
    ssq_recv[tp] = ssq[...]
    each_tp(lambda d: ssq_copy(d, tp).start())

    bc_halo.wait_send()
    x_halo.wait_send()
    each_peer(lambda d: lam_copy(d, d).wait_send())
    each_peer(lambda d: part_copy(d, d).wait_send())
    each_peer(lambda d: start_copy(d, d).wait_send())
    each_tp(lambda s: ssq_copy(s, s).wait_recv())
    ssq_ref[...] = jnp.sum(ssq_recv[...], axis=0)
    each_tp(lambda d: ssq_copy(d, d).wait_send())

    def out_done(c, _):
        out_copy(c).wait()
        return 0

    lax.fori_loop(0, chunks, out_done, 0)


def norm(count, per_step, g_ref, ssq_ref, gain_ref, out_ref):
    for k in range(per_step):
        at = pl.program_id(0) * per_step + k
        row = lax.rsqrt(ssq_ref[pl.ds(at, 1), :] * (1.0 / count) + 1e-5)
        column = jnp.broadcast_to(row, (CHUNK, CHUNK)).T
        for lane in range(0, g_ref.shape[1], 128):
            here = (slice(k * CHUNK, (k + 1) * CHUNK), slice(lane, lane + 128))
            out_ref[here] = (g_ref[here].astype(F32) * column * gain_ref[:, lane : lane + 128]).astype(BF16)


def per_device(
    x_raw, bc_raw, z_gate, conv_x, conv_bc, step_size, log_decay, skip_scale, norm_gain, *, ctx_size, tp_size
):
    length, channels = x_raw.shape
    heads = step_size.shape[1]
    head_dim = channels // heads
    n_state = bc_raw.shape[1] // 2
    chunks = length // CHUNK
    groups = channels // GROUP
    part_rows = n_state * groups // ctx_size
    anywhere = pl.BlockSpec(memory_space=pl.ANY)
    in_vmem = pl.BlockSpec(memory_space=pltpu.VMEM)
    vmem = pltpu.VMEM
    dma = pltpu.SemaphoreType.DMA
    gated, squares = pl.pallas_call(
        functools.partial(mixer, ctx_size, tp_size, head_dim),
        out_shape=(
            jax.ShapeDtypeStruct((length, channels), BF16),
            jax.ShapeDtypeStruct((16, 128), F32),
        ),
        in_specs=[anywhere, anywhere, anywhere, in_vmem, in_vmem, anywhere, anywhere, in_vmem],
        out_specs=(anywhere, in_vmem),
        scratch_shapes=[
            vmem((length + HALO, channels), BF16),
            vmem((length + HALO, 2 * n_state), BF16),
            vmem((length, channels), BF16),
            vmem((length, heads), F32),
            vmem((length, heads), F32),
            vmem((3 * heads, channels), BF16),
            vmem((CHUNK, 3 * CHUNK), BF16),
            vmem((length, 2 * heads), BF16),
            vmem((length, 2 * heads), BF16),
            vmem((32, heads), F32),
            vmem((32, channels), F32),
            vmem((chunks, CHUNK, CHUNK + n_state), BF16),
            vmem((chunks, n_state, CHUNK), BF16),
            vmem((length, channels), BF16),
            vmem((chunks, CHUNK + n_state, channels), BF16),
            vmem((n_state, GROUP), F32),
            vmem((ctx_size, part_rows, GROUP), BF16),
            vmem((ctx_size, part_rows, GROUP), BF16),
            vmem((8, 128), F32),
            vmem((ctx_size, 8, 128), F32),
            vmem((ctx_size, GROUP), F32),
            vmem((ctx_size, part_rows, GROUP), BF16),
            vmem((groups, n_state, GROUP), BF16),
            vmem((length, channels), F32),
            vmem((length, channels), BF16),
            vmem((length, channels), BF16),
            vmem((16, 128), F32),
            vmem((tp_size, 16, 128), F32),
            dma((4 + groups,)),
            dma((2,)),
            dma((2,)),
            dma((ctx_size,)),
            dma((ctx_size,)),
            dma((ctx_size,)),
            dma((ctx_size,)),
            dma((ctx_size,)),
            dma((ctx_size,)),
            dma((tp_size,)),
            dma((tp_size,)),
            dma((chunks,)),
        ],
        compiler_params=pltpu.CompilerParams(
            collective_id=0, has_side_effects=True, vmem_limit_bytes=44 * 1024 * 1024
        ),
        name="mixer",
    )(x_raw, bc_raw, z_gate, conv_x, conv_bc, step_size, log_decay, skip_scale.reshape(1, heads))

    per_step = 2
    return pl.pallas_call(
        functools.partial(norm, channels * tp_size, per_step),
        grid=(chunks // per_step,),
        out_shape=jax.ShapeDtypeStruct((length, channels), BF16),
        in_specs=[
            pl.BlockSpec((per_step * CHUNK, channels), lambda i: (i, 0)),
            pl.BlockSpec((16, 128), lambda i: (0, 0)),
            pl.BlockSpec((1, channels), lambda i: (0, 0)),
        ],
        out_specs=pl.BlockSpec((per_step * CHUNK, channels), lambda i: (i, 0)),
        name="norm",
    )(gated, squares, norm_gain.reshape(1, channels))


def solution(mesh):
    sizes = dict(mesh.shape)
    return jax.shard_map(
        functools.partial(per_device, ctx_size=sizes["ctx"], tp_size=sizes["tp"]),
        mesh=mesh,
        in_specs=(
            P("ctx", "tp"),
            P("ctx", None),
            P("ctx", "tp"),
            P(None, "tp"),
            P(),
            P("ctx", "tp"),
            P("ctx", "tp"),
            P("tp"),
            P("tp"),
        ),
        out_specs=P("ctx", "tp"),
        check_vma=False,
    )
```

time: 692 us -> 68.3 us (0.10)
  the two profiles are of different devices: /device:TPU:16 before, /device:TPU:1 now
where the time goes in v1:
time: 68.3 us; the launch traced here: 67.9 us
  Pallas kernels  58.2 us (85%)
  local copies, waits for them, and re-layouts  9.62 us (14%)
    pallas_call x1, Pallas kernels, per_device(): pl.pallas_call(functools.partial(mixer, ctx_size, tp_size, head_dim), out...  52.4 us
    unnamed x16, local copies, waits for them, and re-layouts  9.62 us
    pallas_call x1, Pallas kernels, per_device(): pl.pallas_call(functools.partial(norm, channels * tp_size, per_step), gri...  5.79 us

profile of v1, /device:TPU:1, one launch (start us, length us, event | category | flops | bytes accessed | tf_op | source)
XLA Modules:
  0.0 67.9 jit_solution(9643895404491892195)
XLA Ops:
  0.0 1.2 %copy.10.step_hbm = f32[1536,16]{1,0:T(8,128)S(1)} copy(f32[1536,16]{0,1:T(8,128)} %param.14) | data formatting | bytes 196608 | tf_op args[5]
  1.2 1.2 %copy.11.log_hbm = f32[1536,16]{1,0:T(8,128)S(1)} copy(f32[1536,16]{0,1:T(8,128)} %param.15) | data formatting | bytes 196608 | tf_op args[6]
  2.3 0.0 copy-start
  2.3 1.9 %copy-done = bf16[1536,1024]{1,0:T(8,128)(2,1)S(1)} copy-done((bf16[1536,1024]{1,0:T(8,128)(2,1)S(1)}, bf16[1536,1024]{1,0:T(8,128)(2,1)}, u32[]{:S(2)}) %copy-start) | copy-done | bytes 3145752
  4.2 0.0 copy-start.2
  4.2 1.1 %copy-done.2 = bf16[1536,256]{1,0:T(8,128)(2,1)S(1)} copy-done((bf16[1536,256]{1,0:T(8,128)(2,1)S(1)}, bf16[1536,256]{1,0:T(8,128)(2,1)}, u32[]{:S(2)}) %copy-start.2) | copy-done | bytes 786456
  5.4 0.0 copy-start.3
  5.4 0.7 %copy-done.3 = f32[4,1024]{1,0:T(4,128)S(1)} copy-done((f32[4,1024]{1,0:T(4,128)S(1)}, f32[4,1024]{1,0:T(4,128)}, u32[]{:S(2)}) %copy-start.3) | copy-done | bytes 16408
  6.1 0.0 copy-start.5
  6.1 0.7 %copy-done.5 = f32[4,256]{1,0:T(4,128)S(1)} copy-done((f32[4,256]{1,0:T(4,128)S(1)}, f32[4,256]{1,0:T(4,128)}, u32[]{:S(2)}) %copy-start.5) | copy-done | bytes 4120
  6.8 0.0 copy-start.6
  6.8 0.7 copy-done.6
  7.4 52.4 %mixer.1 = (bf16[1536,1024]{1,0:T(8,128)(2,1)S(1)}, f32[16,128]{1,0:T(8,128)S(1)}) custom-call(bf16[1536,1024]{1,0:T(8,128)(2,1)S(1)} %copy-done, bf16[1536,256]{1,0:T(8,128)(2,1)S(1)} %copy-done.2, bf16[1536,1024]{1,0:T(8,128)(2,1)} %z_hbm.1, f32[4,1024]{1,0:T(4,128)S(1)} %copy-done.3, f32[4,256]{1,0:T(4,128)S(1)} %copy-done.5, ...), custom_call_target="tpu_custom_call" | custom-call | tf_op jit(solution)/shard_map/mixer/pallas_call | solution.py:367
  59.8 0.0 copy-start.1
  59.8 1.6 %copy-done.1 = bf16[1536,1024]{1,0:T(8,128)(2,1)} copy-done((bf16[1536,1024]{1,0:T(8,128)(2,1)}, bf16[1536,1024]{1,0:T(8,128)(2,1)S(1)}, u32[]{:S(2)}) %copy-start.1) | copy-done | bytes 3145752
  61.5 0.0 copy-start.4
  61.5 0.6 copy-done.4
  62.1 5.8 %norm.1 = bf16[1536,1024]{1,0:T(8,128)(2,1)} custom-call(bf16[1536,1024]{1,0:T(8,128)(2,1)} %copy-done.1, f32[16,128]{1,0:T(8,128)} %copy-done.4, f32[1,1024]{1,0:T(1,128)} %bitcast.3), custom_call_target="tpu_custom_call" | custom-call | tf_op jit(solution)/shard_map/norm/pallas_call | solution.py:424
Async XLA Ops:
  2.3 1.9 %copy-start = (bf16[1536,1024]{1,0:T(8,128)(2,1)S(1)}, bf16[1536,1024]{1,0:T(8,128)(2,1)}, u32[]{:S(2)}) copy-start(bf16[1536,1024]{1,0:T(8,128)(2,1)} %x_hbm.1) | copy-start | bytes 9437188
  4.2 1.1 %copy-start.2 = (bf16[1536,256]{1,0:T(8,128)(2,1)S(1)}, bf16[1536,256]{1,0:T(8,128)(2,1)}, u32[]{:S(2)}) copy-start(bf16[1536,256]{1,0:T(8,128)(2,1)} %bc_hbm.1) | copy-start | bytes 2359300
  5.4 0.7 %copy-start.3 = (f32[4,1024]{1,0:T(4,128)S(1)}, f32[4,1024]{1,0:T(4,128)}, u32[]{:S(2)}) copy-start(f32[4,1024]{1,0:T(4,128)} %convx_ref.1) | copy-start | bytes 49156
  6.1 0.7 %copy-start.5 = (f32[4,256]{1,0:T(4,128)S(1)}, f32[4,256]{1,0:T(4,128)}, u32[]{:S(2)}) copy-start(f32[4,256]{1,0:T(4,128)} %convbc_ref.1) | copy-start | bytes 12292
  6.8 0.7 copy-start.6
  59.8 1.6 %copy-start.1 = (bf16[1536,1024]{1,0:T(8,128)(2,1)}, bf16[1536,1024]{1,0:T(8,128)(2,1)S(1)}, u32[]{:S(2)}) copy-start(bf16[1536,1024]{1,0:T(8,128)(2,1)S(1)} %get-tuple-element.7.g_ref) | copy-start | bytes 9437188
  61.5 0.6 copy-start.4

commit v2 on v0

v2 whole, which is shorter than its diff:
```python
import functools

import jax
import jax.numpy as jnp
from jax import lax
from jax.experimental import pallas as pl
from jax.experimental.pallas import tpu as pltpu
from jax.sharding import PartitionSpec as P

F32 = jnp.float32
BF16 = jnp.bfloat16
MESH = pl.DeviceIdType.MESH
CHUNK = 128
LANES = 128
GROUP = 256
TILES = GROUP // LANES
HALO = 16
BATCH = 4
PAIR = 2


def split3(value):
    high = value.astype(BF16)
    rest = value - high.astype(F32)
    mid = rest.astype(BF16)
    return high, mid, (rest - mid.astype(F32)).astype(BF16)


def silu_of_half(half):
    return half * jnp.tanh(half) + half


def dot(left, right):
    return jnp.dot(left, right, preferred_element_type=F32)


def mixer(
    ctx_size, tp_size, head_dim,
    x_hbm, bc_hbm, z_hbm, convx_hbm, convbc_hbm, step_hbm, log_hbm, skip_hbm, gain_hbm,
    out_hbm,
    xbuf, bcbuf, zbuf, stepbuf, logbuf, convx_ref, convbc_ref, skip_ref, gain_ref,
    spread, factor_map, shift_one, shift_all, shift_rim, sums, factors, rows_ref,
    scores_ref, c_ref, bt, xconv, xs, state, parts, recv, lam_wide, send, start_state,
    ahead, local_ref, gate_ref, squares, ssq, ssq_recv, inverse,
    load_sem, halo_send, halo_recv, part_send, part_recv, start_send, start_recv, ssq_send, ssq_recv_sem,
    out_sem,
):
    length, channels = x_hbm.shape
    heads = step_hbm.shape[0]
    chunks = length // CHUNK
    groups = channels // GROUP
    n_state = bt.shape[1]
    part_rows = parts.shape[2]
    per_group = ctx_size // groups
    mid = CHUNK // 2 - 1
    me = lax.axis_index("ctx")
    tp = lax.axis_index("tp")
    mine = lax.rem(me, groups)
    my_row = pl.multiple_of((me // groups) * part_rows, part_rows)

    def wide(ref, g, *at):
        return jnp.concatenate([ref[(g * TILES + k, *at)] for k in range(TILES)], axis=-1)

    def put(ref, g, at, value):
        for k in range(TILES):
            ref[(g * TILES + k, *at)] = value[:, k * LANES : (k + 1) * LANES]

    def rows_of(c):
        return pl.ds(pl.multiple_of(c * CHUNK, CHUNK), CHUNK)

    small_loads = [
        pltpu.make_async_copy(src, dst, load_sem.at[k])
        for k, (src, dst) in enumerate(
            (
                (log_hbm, logbuf),
                (step_hbm, stepbuf),
                (skip_hbm, skip_ref),
                (convbc_hbm, convbc_ref),
                (convx_hbm, convx_ref),
                (gain_hbm, gain_ref),
            )
        )
    ]
    bc_loads = [
        pltpu.make_async_copy(
            bc_hbm.at[:, pl.ds(k * LANES, LANES)], bcbuf.at[k, pl.ds(HALO, length)], load_sem.at[6 + k]
        )
        for k in range(2)
    ]

    def x_load(k):
        col = pl.ds(pl.multiple_of(k * LANES, LANES), LANES)
        return pltpu.make_async_copy(x_hbm.at[:, col], xbuf.at[k, pl.ds(HALO, length)], load_sem.at[8 + k])

    def z_load(k):
        col = pl.ds(pl.multiple_of(k * LANES, LANES), LANES)
        return pltpu.make_async_copy(
            z_hbm.at[:, col], zbuf.at[k], load_sem.at[8 + groups * TILES + k]
        )

    for load in small_loads + bc_loads:
        load.start()
    for k in range(groups * TILES):
        x_load(k).start()
    for k in range(groups * TILES):
        z_load(k).start()

    barrier = pltpu.get_barrier_semaphore()

    def greet_ctx(k, _):
        pl.semaphore_signal(barrier, inc=1, device_id=(lax.rem(me + k, ctx_size), tp), device_id_type=MESH)
        return 0

    def greet_tp(k, _):
        pl.semaphore_signal(barrier, inc=1, device_id=(me, lax.rem(tp + k, tp_size)), device_id_type=MESH)
        return 0

    lax.fori_loop(1, ctx_size, greet_ctx, 0)
    lax.fori_loop(1, tp_size, greet_tp, 0)

    s_at = lax.broadcasted_iota(jnp.int32, (CHUNK, CHUNK), 0)
    t_at = lax.broadcasted_iota(jnp.int32, (CHUNK, CHUNK), 1)
    upto = jnp.where(s_at <= t_at, 1.0, 0.0)
    sums[0] = (upto - jnp.where(s_at <= mid, 1.0, 0.0)).astype(BF16)
    sums[1] = upto.astype(BF16)
    sums[2] = jnp.ones((CHUNK, CHUNK), BF16)

    head_at = lax.broadcasted_iota(jnp.int32, (heads, channels), 0)
    channel_at = lax.broadcasted_iota(jnp.int32, (heads, channels), 1)
    first = head_at * head_dim
    one_map = jnp.where((channel_at >= first) & (channel_at < first + head_dim), 1.0, 0.0).astype(BF16)
    factor_map[...] = jnp.zeros_like(factor_map)
    for k in range(3):
        spread[k * heads : (k + 1) * heads, :] = one_map
        for term in range(2):
            row = (2 * k + term) * heads
            for lane in range(groups * TILES):
                factor_map[k, lane, row : row + heads, :] = one_map[:, lane * LANES : (lane + 1) * LANES]

    def shift(by, width, before):
        to = lax.broadcasted_iota(jnp.int32, (CHUNK, width), 0)
        at = lax.broadcasted_iota(jnp.int32, (CHUNK, width), 1)
        return jnp.where(to + (before - by) == at, 1.0, 0.0).astype(BF16)

    for by in range(4):
        shift_all[by] = shift(by, CHUNK, 0)
        if by > 0:
            shift_one[(by - 1) * CHUNK : by * CHUNK, :] = shift(by, CHUNK + HALO, HALO)
    halo_to = lax.broadcasted_iota(jnp.int32, (CHUNK, 3 * HALO), 0)
    halo_at = lax.broadcasted_iota(jnp.int32, (CHUNK, 3 * HALO), 1)
    halo_hit = halo_to < 0
    for by in range(1, 4):
        inside = (halo_at >= (by - 1) * HALO) & (halo_at < by * HALO)
        halo_hit = halo_hit | ((halo_to + (by * HALO - by) == halo_at) & inside)
    shift_rim[...] = jnp.where(halo_hit, 1.0, 0.0).astype(BF16)

    for load in small_loads:
        load.wait()

    def decays(b, carry):
        before, windows = carry
        batch = [b * BATCH + k for k in range(BATCH)]
        window = lax.broadcasted_iota(jnp.int32, (CHUNK, CHUNK), 1) * CHUNK + mid
        results = []
        for c in batch:
            pieces = jnp.concatenate(split3(logbuf[:, rows_of(c)]), axis=0)
            token = lax.broadcasted_iota(jnp.int32, (CHUNK, CHUNK), 0) + c * CHUNK
            hit = ((token <= window) & (token > window - CHUNK)) | (window == 15 * CHUNK + mid)
            matrix = jnp.concatenate((sums[0], sums[1], sums[2], jnp.where(hit, 1.0, 0.0).astype(BF16)), axis=1)
            result = dot(pieces, matrix)
            results.append(result[:heads] + result[heads : 2 * heads] + result[2 * heads :])
        for c, result in zip(batch, results):
            centred = result[:, :CHUNK]
            values = []
            for value in (
                jnp.exp(-centred) * stepbuf[:, rows_of(c)],
                jnp.exp(centred),
                jnp.exp(before + result[:, CHUNK : 2 * CHUNK]),
            ):
                high = value.astype(BF16).astype(F32)
                values += [high, value - high]
            factors[c] = jnp.concatenate(values, axis=0).T.astype(BF16)
            before = before + result[:, 2 * CHUNK : 3 * CHUNK]
            windows = windows + result[:, 3 * CHUNK :]
        return before, windows

    none = jnp.zeros((heads, CHUNK), F32)
    _, windows = lax.fori_loop(0, chunks // BATCH, decays, (none, none))
    head_rows = jnp.exp(windows).T[:16]
    lam_row = jnp.concatenate(split3(head_rows[15:16]) + (jnp.zeros((1, LANES - 3 * heads), BF16),), axis=1)
    lam_tile = jnp.broadcast_to(lam_row.astype(F32), (part_rows, LANES)).astype(BF16)

    def put_lam(d, _):
        parts[d, TILES] = lam_tile
        return 0

    lax.fori_loop(0, ctx_size, put_lam, 0)
    row_at = lax.broadcasted_iota(jnp.int32, (16, heads), 0)
    head_rows = jnp.where(row_at == 14, skip_ref[...], head_rows)
    head_rows = dot(jnp.concatenate(split3(head_rows), axis=1), spread[...])
    for lane in range(groups * TILES):
        rows_ref[lane] = head_rows[:, lane * LANES : (lane + 1) * LANES]

    pl.semaphore_wait(barrier, ctx_size + tp_size - 2)

    right = lax.rem(me + 1, ctx_size)

    def halo_copy(src, dst, at):
        return pltpu.make_async_remote_copy(
            src_ref=src, dst_ref=dst, send_sem=halo_send.at[at], recv_sem=halo_recv.at[at],
            device_id=(right, tp), device_id_type=MESH,
        )

    halos = [
        halo_copy(bcbuf.at[:, pl.ds(length, HALO)], bcbuf.at[:, pl.ds(0, HALO)], 0),
        halo_copy(xbuf.at[:, pl.ds(length, HALO)], xbuf.at[:, pl.ds(0, HALO)], 1),
    ]

    def part_copy(src, dst, to):
        return pltpu.make_async_remote_copy(
            src_ref=src, dst_ref=dst, send_sem=part_send.at[0], recv_sem=part_recv.at[0],
            device_id=(to, tp), device_id_type=MESH,
        )

    def start_copy(src, dst, to):
        return pltpu.make_async_remote_copy(
            src_ref=src, dst_ref=dst, send_sem=start_send.at[0], recv_sem=start_recv.at[0],
            device_id=(to, tp), device_id_type=MESH,
        )

    def ssq_copy(dst, src):
        return pltpu.make_async_remote_copy(
            src_ref=ssq, dst_ref=ssq_recv.at[src], send_sem=ssq_send.at[dst],
            recv_sem=ssq_recv_sem.at[src], device_id=(me, dst), device_id_type=MESH,
        )

    def each_tp(fn):
        def step(k, _):
            fn(lax.rem(tp + k, tp_size))
            return 0

        lax.fori_loop(1, tp_size, step, 0)

    others = pl.ds(0, ctx_size - 1)
    all_parts = part_copy(parts.at[others], recv.at[others], right)
    all_starts = start_copy(send.at[others], send.at[others], right)

    for load in bc_loads:
        load.wait()
    halos[0].start()

    bc_taps = [0.5 * convbc_ref[k : k + 1, :] for k in range(4)]

    def project(b):
        batch = [b * BATCH + k for k in range(BATCH)]
        blocks, moved = [], []
        for c in batch:
            rows = pl.ds(pl.multiple_of(c * CHUNK, CHUNK), CHUNK + HALO)
            blocks.append(jnp.concatenate((bcbuf[0, rows], bcbuf[1, rows]), axis=1))
        for block in blocks:
            moved.append(dot(shift_one[...], block))
        turned, c_rows = [], []
        for c, block, move in zip(batch, blocks, moved):
            half = bc_taps[3] * block[HALO:].astype(F32)
            for by in range(1, 4):
                half = half + bc_taps[3 - by] * move[(by - 1) * CHUNK : by * CHUNK]
            both = silu_of_half(half).astype(BF16)
            c_rows.append(both[:, n_state:])
            turned.append(both[:, :n_state].T)
            bt[c] = turned[-1]
            c_ref[c] = c_rows[-1]
        causal = lax.broadcasted_iota(jnp.int32, (CHUNK, CHUNK), 0) >= lax.broadcasted_iota(
            jnp.int32, (CHUNK, CHUNK), 1
        )
        scores = [dot(c_row, b_turned) for c_row, b_turned in zip(c_rows, turned)]
        for c, score in zip(batch, scores):
            scores_ref[c] = jnp.where(causal, score, 0.0).astype(BF16)

    def project_step(b, _):
        @pl.when(b == 0)
        def _():
            for k in range(groups * TILES):
                x_load(k).wait()
            halos[1].start()
            for halo, ref in zip(halos, (bcbuf, xbuf)):
                halo.wait_recv()
                for k in range(ref.shape[0]):
                    ref[k, 0:HALO] = jnp.where(me > 0, ref[k, 0:HALO].astype(F32), 0.0).astype(BF16)

        project(b)
        return 0

    last = chunks // BATCH - 1
    lax.fori_loop(0, chunks // BATCH, lambda k, v: project_step(last - k, v), 0)

    def carry_through():
        all_parts.wait_recv()
        col = pl.multiple_of(mine * GROUP, GROUP)
        decay = recv[:, TILES].reshape(ctx_size * part_rows, LANES)[:, : 3 * heads]
        decay = dot(decay, spread[:, pl.ds(col, GROUP)])
        lam_wide[...] = decay.reshape(ctx_size, part_rows, GROUP)

        def step(d, running):
            for k in range(TILES):
                send[d, k] = running[:, k * LANES : (k + 1) * LANES].astype(BF16)
            arrived = jnp.concatenate([recv[d, k] for k in range(TILES)], axis=1)
            return lam_wide[d] * running + arrived.astype(F32)

        lax.fori_loop(0, ctx_size, step, jnp.zeros((part_rows, GROUP), F32), unroll=4)
        here = start_state.at[pl.ds(mine * TILES, TILES), pl.ds(my_row, part_rows)]
        start_state[pl.ds(mine * TILES, TILES), pl.ds(my_row, part_rows)] = send[me]

        def send_start(k, _):
            to = lax.rem(me + k, ctx_size)
            start_copy(send.at[to], here, to).start()
            return 0

        lax.fori_loop(1, ctx_size, send_start, 0)

    batches = chunks // BATCH

    def tap_sums(u):
        g, b = lax.div(u, batches), lax.rem(u, batches)
        col = pl.ds(pl.multiple_of(g * GROUP, GROUP), GROUP)
        taps = [(0.5 * convx_ref[k : k + 1, col]).astype(BF16) for k in range(4)]
        shifts = jnp.concatenate([shift_all[by] for by in range(4)] + [shift_rim[...]], axis=1)

        def one(k):
            at = pl.multiple_of((b * BATCH + k) * CHUNK, CHUNK)
            block = wide(xbuf, g, pl.ds(at, CHUNK + HALO))
            terms = [block * taps[3 - by] for by in range(1, 4)]
            stacked = jnp.concatenate(
                [block[HALO:] * taps[3]] + [term[HALO:] for term in terms] + [term[:HALO] for term in terms], axis=0
            )
            return dot(shifts, stacked)

        return one

    def forward(u, _):
        g, b = lax.div(u, batches), lax.rem(u, batches)
        batch = [b * BATCH + k for k in range(BATCH)]
        factor = factors[pl.ds(b * BATCH, BATCH)].reshape(BATCH * CHUNK, 6 * heads)
        scales = dot(factor, wide(factor_map.at[0], g, slice(None)))
        next_sums = tap_sums(lax.rem(u + 1, groups * batches))
        scaled = []
        for k, c in enumerate(batch):
            value = silu_of_half(ahead[k])
            ahead[k] = next_sums(k)
            put(xconv, g, (rows_of(c),), value.astype(BF16))
            scaled.append((value * scales[k * CHUNK : (k + 1) * CHUNK]).astype(BF16))
            put(xs, g, (c, slice(0, CHUNK)), scaled[-1])
        added = [dot(bt[c], value) for c, value in zip(batch, scaled)]
        held = jnp.where(b == 0, 0.0, state[...])
        for c, more in zip(batch, added):
            put(xs, g, (c, slice(CHUNK, CHUNK + n_state)), held.astype(BF16))
            held = wide(rows_ref, g, pl.ds(c + 1, 1)) * (held + more)
        state[...] = held

        @pl.when(b == batches - 1)
        def _():
            for r in range(per_group):
                for k in range(TILES):
                    parts[r * groups + g, k] = state[
                        r * part_rows : (r + 1) * part_rows, k * LANES : (k + 1) * LANES
                    ].astype(BF16)

            @pl.when(mine == g)
            def _():
                recv[me] = parts[me]

            def send_part(k, _):
                to = lax.rem(me // groups + k, per_group) * groups + g

                @pl.when(to != me)
                def _():
                    part_copy(parts.at[to], recv.at[me], to).start()

                return 0

            lax.fori_loop(0, per_group, send_part, 0)
            pl.when(mine == g - 1)(carry_through)

        return 0

    first_sums = tap_sums(jnp.int32(0))
    for k in range(BATCH):
        ahead[k] = first_sums(k)
    lax.fori_loop(0, groups * batches, forward, 0)

    for k in range(groups * TILES):
        z_load(k).wait()

    def local(b, _):
        batch = [b * PAIR + k for k in range(PAIR)]
        factor = factors[pl.ds(b * PAIR, PAIR)].reshape(PAIR * CHUNK, 6 * heads)
        for g in range(groups):
            inner = [
                dot(
                    jnp.concatenate((scores_ref[c], c_ref[c]), axis=1),
                    wide(xs, g, c),
                )
                for c in batch
            ]
            scales = dot(factor, wide(factor_map.at[1], g, slice(None)))
            reaches = dot(factor, wide(factor_map.at[2], g, slice(None)))
            skip = wide(rows_ref, g, slice(14, 15))
            for k, c in enumerate(batch):
                part = slice(k * CHUNK, (k + 1) * CHUNK)
                gate = silu_of_half((wide(zbuf, g, rows_of(c)) * 0.5).astype(F32))
                skipped = skip * wide(xconv, g, rows_of(c)).astype(F32)
                put(local_ref, g, (rows_of(c),), (inner[k] * scales[part] + skipped) * gate)
                put(gate_ref, g, (rows_of(c),), (reaches[part] * gate).astype(BF16))
        return 0

    half_way = chunks // PAIR // 2
    lax.fori_loop(0, half_way, local, 0)
    pl.when(mine == groups - 1)(carry_through)
    lax.fori_loop(half_way, chunks // PAIR, local, 0)

    all_starts.wait_recv()
    ssq[...] = jnp.zeros_like(ssq)

    def finish(b, _):
        batch = [b * PAIR + k for k in range(PAIR)]
        c_rows = c_ref[pl.ds(b * PAIR, PAIR)].reshape(PAIR * CHUNK, n_state)
        total = [jnp.zeros((CHUNK, LANES), F32) for _ in batch]
        for g in range(groups):
            carried = dot(c_rows, wide(start_state, g, slice(None)))
            for k, c in enumerate(batch):
                gated = wide(local_ref, g, rows_of(c)) + wide(gate_ref, g, rows_of(c)).astype(F32) * carried[
                    k * CHUNK : (k + 1) * CHUNK
                ]
                put(local_ref, g, (rows_of(c),), gated)
                both = gated * gated
                for lane in range(0, GROUP, LANES):
                    total[k] = total[k] + both[:, lane : lane + LANES]
        for k, c in enumerate(batch):
            squares[c] = total[k]
        return 0

    lax.fori_loop(0, chunks // PAIR, finish, 0)

    def turn(b, _):
        for c in [b * BATCH + k for k in range(BATCH)]:
            ssq[pl.ds(c, 1), :] = jnp.sum(squares[c].T, axis=0, keepdims=True)
        return 0

    lax.fori_loop(0, chunks // BATCH, turn, 0)
    ssq_recv[tp] = ssq[...]
    each_tp(lambda d: ssq_copy(d, tp).start())

    for halo in halos:
        halo.wait_send()
    all_parts.wait_send()
    all_starts.wait_send()
    each_tp(lambda s: ssq_copy(s, s).wait_recv())
    mean = jnp.sum(ssq_recv[...], axis=0) * (1.0 / (channels * tp_size))
    inverse[...] = lax.rsqrt(mean + 1e-5)
    each_tp(lambda d: ssq_copy(d, d).wait_send())

    def out_copy(b, lane):
        rows = pl.ds(pl.multiple_of(b * BATCH * CHUNK, CHUNK), BATCH * CHUNK)
        return pltpu.make_async_copy(
            zbuf.at[lane, rows], out_hbm.at[rows, pl.ds(lane * LANES, LANES)], out_sem.at[b, lane]
        )

    def norm(b, _):
        columns = [
            jnp.broadcast_to(inverse[pl.ds(b * BATCH + k, 1), :], (CHUNK, CHUNK)).T for k in range(BATCH)
        ]
        for lane in range(groups * TILES):
            gain = gain_ref[:, lane * LANES : (lane + 1) * LANES]
            for k in range(BATCH):
                at = rows_of(b * BATCH + k)
                zbuf[lane, at] = (local_ref[lane, at] * columns[k] * gain).astype(BF16)
        for lane in range(groups * TILES):
            out_copy(b, lane).start()
        return 0

    lax.fori_loop(0, batches, norm, 0)

    def norm_done(b, _):
        for lane in range(groups * TILES):
            out_copy(b, lane).wait()
        return 0

    lax.fori_loop(0, batches, norm_done, 0)


def per_device(
    x_raw, bc_raw, z_gate, conv_x, conv_bc, step_size, log_decay, skip_scale, norm_gain, *, ctx_size, tp_size
):
    length, channels = x_raw.shape
    heads = step_size.shape[1]
    head_dim = channels // heads
    n_state = bc_raw.shape[1] // 2
    chunks = length // CHUNK
    groups = channels // GROUP
    lanes = channels // LANES
    part_rows = n_state * groups // ctx_size
    in_hbm = pl.BlockSpec(memory_space=pltpu.HBM)
    vmem = pltpu.VMEM
    dma = pltpu.SemaphoreType.DMA
    return pl.pallas_call(
        functools.partial(mixer, ctx_size, tp_size, head_dim),
        out_shape=jax.ShapeDtypeStruct((length, channels), BF16),
        in_specs=[in_hbm] * 9,
        out_specs=in_hbm,
        scratch_shapes=[
            vmem((lanes, length + HALO, LANES), BF16),
            vmem((2, length + HALO, n_state), BF16),
            vmem((lanes, length, LANES), BF16),
            vmem((heads, length), F32),
            vmem((heads, length), F32),
            vmem((4, channels), F32),
            vmem((4, 2 * n_state), F32),
            vmem((1, heads), F32),
            vmem((1, channels), F32),
            vmem((3 * heads, channels), BF16),
            vmem((3, lanes, 6 * heads, LANES), BF16),
            vmem((3 * CHUNK, CHUNK + HALO), BF16),
            vmem((4, CHUNK, CHUNK), BF16),
            vmem((CHUNK, 3 * HALO), BF16),
            vmem((3, CHUNK, CHUNK), BF16),
            vmem((chunks, CHUNK, 6 * heads), BF16),
            vmem((lanes, 16, LANES), F32),
            vmem((chunks, CHUNK, CHUNK), BF16),
            vmem((chunks, CHUNK, n_state), BF16),
            vmem((chunks, n_state, CHUNK), BF16),
            vmem((lanes, length, LANES), BF16),
            vmem((lanes, chunks, CHUNK + n_state, LANES), BF16),
            vmem((n_state, GROUP), F32),
            vmem((ctx_size, TILES + 1, part_rows, LANES), BF16),
            vmem((ctx_size, TILES + 1, part_rows, LANES), BF16),
            vmem((ctx_size, part_rows, GROUP), F32),
            vmem((ctx_size, TILES, part_rows, LANES), BF16),
            vmem((lanes, n_state, LANES), BF16),
            vmem((BATCH, CHUNK, GROUP), F32),
            vmem((lanes, length, LANES), F32),
            vmem((lanes, length, LANES), BF16),
            vmem((chunks, CHUNK, LANES), F32),
            vmem((16, 128), F32),
            vmem((tp_size, 16, 128), F32),
            vmem((16, 128), F32),
            dma((8 + 2 * lanes,)),
            dma((2,)),
            dma((2,)),
            dma((1,)),
            dma((1,)),
            dma((1,)),
            dma((1,)),
            dma((tp_size,)),
            dma((tp_size,)),
            dma((chunks // BATCH, lanes)),
        ],
        compiler_params=pltpu.CompilerParams(
            collective_id=0, has_side_effects=True, vmem_limit_bytes=56 * 1024 * 1024
        ),
        name="mixer",
    )(
        x_raw, bc_raw, z_gate, conv_x, conv_bc, step_size.T, log_decay.T,
        skip_scale.reshape(1, heads), norm_gain.reshape(1, channels),
    )


def solution(mesh):
    sizes = dict(mesh.shape)
    return jax.shard_map(
        functools.partial(per_device, ctx_size=sizes["ctx"], tp_size=sizes["tp"]),
        mesh=mesh,
        in_specs=(
            P("ctx", "tp"),
            P("ctx", None),
            P("ctx", "tp"),
            P(None, "tp"),
            P(),
            P("ctx", "tp"),
            P("ctx", "tp"),
            P("tp"),
            P("tp"),
        ),
        out_specs=P("ctx", "tp"),
        check_vma=False,
    )
```

time: 692 us -> 49 us (0.07)
  the two profiles are of different devices: /device:TPU:16 before, /device:TPU:1 now
where the time goes in v2:
time: 49 us; the launch traced here: 48.9 us
  Pallas kernels  45 us (92%)
  local copies, waits for them, and re-layouts  3.86 us (8%)
    pallas_call x1, Pallas kernels, per_device(): pl.pallas_call(functools.partial(mixer, ctx_size, tp_size, head_dim), out...  45 us
    unnamed x1, local copies, waits for them, and re-layouts  3.86 us

profile of v2, /device:TPU:1, one launch (start us, length us, event | category | flops | bytes accessed | tf_op | source)
XLA Modules:
  0.0 48.9 jit_solution(11311961804818965189)
XLA Ops:
  0.0 45.0 %mixer.1 = bf16[1536,1024]{1,0:T(8,128)(2,1)} custom-call(bf16[1536,1024]{1,0:T(8,128)(2,1)} %x_hbm.1, bf16[1536,256]{1,0:T(8,128)(2,1)} %bc_hbm.1, bf16[1536,1024]{1,0:T(8,128)(2,1)} %z_hbm.1, f32[4,1024]{1,0:T(4,128)} %convx_hbm.1, f32[4,256]{1,0:T(4,128)} %convbc_hbm.1, f32[16,1536]{1,0:T(8,128)} %bitcast.4, f32[16,1536]{1,0:T(8,128)} %bitcast.5, ...), custom_call_target="tpu_custom_call" | custom-call | tf_op jit(solution)/shard_map/mixer/pallas_call | solution.py:504
  45.0 3.9 %copy.11 = bf16[1536,1024]{1,0:T(8,128)(2,1)} copy(bf16[1536,1024]{1,0:T(8,128)(2,1)} %mixer.1) | data formatting | bytes 6291456

commit v3 on v2

--- a/solution.py
+++ b/solution.py
@@ -34,16 +34,28 @@
     return jnp.dot(left, right, preferred_element_type=F32)
 
 
+def each_other(size, fn):
+    count = size - 1
+    unroll = next(n for n in (6, 5, 4, 3, 2, 1) if (count - 1) % n == 0)
+
+    def step(k, _):
+        fn(k)
+        return 0
+
+    if count > 1:
+        lax.fori_loop(1, count, step, 0, unroll=unroll)
+    fn(count)
+
+
 def mixer(
     ctx_size, tp_size, head_dim,
     x_hbm, bc_hbm, z_hbm, convx_hbm, convbc_hbm, step_hbm, log_hbm, skip_hbm, gain_hbm,
-    out_hbm,
-    xbuf, bcbuf, zbuf, stepbuf, logbuf, convx_ref, convbc_ref, skip_ref, gain_ref,
+    out_ref,
+    xbuf, bcbuf, zbuf, x_rim, bc_rim, stepbuf, logbuf, convx_ref, convbc_ref, skip_ref, gain_ref,
     spread, factor_map, shift_one, shift_all, shift_rim, sums, factors, rows_ref,
     scores_ref, c_ref, bt, xconv, xs, state, parts, recv, lam_wide, send, start_state,
-    ahead, local_ref, gate_ref, squares, ssq, ssq_recv, inverse,
+    ahead, local_ref, gate_ref, squares, ssq, ssq_recv,
     load_sem, halo_send, halo_recv, part_send, part_recv, start_send, start_recv, ssq_send, ssq_recv_sem,
-    out_sem,
 ):
     length, channels = x_hbm.shape
     heads = step_hbm.shape[0]
@@ -107,16 +119,28 @@
 
     barrier = pltpu.get_barrier_semaphore()
 
-    def greet_ctx(k, _):
+    def greet_ctx(k):
         pl.semaphore_signal(barrier, inc=1, device_id=(lax.rem(me + k, ctx_size), tp), device_id_type=MESH)
-        return 0
-
-    def greet_tp(k, _):
+
+    def greet_tp(k):
         pl.semaphore_signal(barrier, inc=1, device_id=(me, lax.rem(tp + k, tp_size)), device_id_type=MESH)
-        return 0
-
-    lax.fori_loop(1, ctx_size, greet_ctx, 0)
-    lax.fori_loop(1, tp_size, greet_tp, 0)
+
+    each_other(ctx_size, greet_ctx)
+    each_other(tp_size, greet_tp)
+
+    pl.semaphore_wait(barrier, ctx_size + tp_size - 2)
+
+    right = lax.rem(me + 1, ctx_size)
+
+    def halo_copy(src, dst, at):
+        return pltpu.make_async_remote_copy(
+            src_ref=src.at[pl.ds(length - HALO, HALO)], dst_ref=dst, send_sem=halo_send.at[at],
+            recv_sem=halo_recv.at[at], device_id=(right, tp), device_id_type=MESH,
+        )
+
+    halos = [halo_copy(bc_hbm, bc_rim, 0), halo_copy(x_hbm, x_rim, 1)]
+    for halo in halos:
+        halo.start()
 
     s_at = lax.broadcasted_iota(jnp.int32, (CHUNK, CHUNK), 0)
     t_at = lax.broadcasted_iota(jnp.int32, (CHUNK, CHUNK), 1)
@@ -194,28 +218,13 @@
         parts[d, TILES] = lam_tile
         return 0
 
-    lax.fori_loop(0, ctx_size, put_lam, 0)
+    lax.fori_loop(0, ctx_size, put_lam, 0, unroll=4)
     row_at = lax.broadcasted_iota(jnp.int32, (16, heads), 0)
     head_rows = jnp.where(row_at == 14, skip_ref[...], head_rows)
     head_rows = dot(jnp.concatenate(split3(head_rows), axis=1), spread[...])
     for lane in range(groups * TILES):
         rows_ref[lane] = head_rows[:, lane * LANES : (lane + 1) * LANES]
 
-    pl.semaphore_wait(barrier, ctx_size + tp_size - 2)
-
-    right = lax.rem(me + 1, ctx_size)
-
-    def halo_copy(src, dst, at):
-        return pltpu.make_async_remote_copy(
-            src_ref=src, dst_ref=dst, send_sem=halo_send.at[at], recv_sem=halo_recv.at[at],
-            device_id=(right, tp), device_id_type=MESH,
-        )
-
-    halos = [
-        halo_copy(bcbuf.at[:, pl.ds(length, HALO)], bcbuf.at[:, pl.ds(0, HALO)], 0),
-        halo_copy(xbuf.at[:, pl.ds(length, HALO)], xbuf.at[:, pl.ds(0, HALO)], 1),
-    ]
-
     def part_copy(src, dst, to):
         return pltpu.make_async_remote_copy(
             src_ref=src, dst_ref=dst, send_sem=part_send.at[0], recv_sem=part_recv.at[0],
@@ -228,18 +237,18 @@
             device_id=(to, tp), device_id_type=MESH,
         )
 
-    def ssq_copy(dst, src):
+    def ssq_copy(p, to):
         return pltpu.make_async_remote_copy(
-            src_ref=ssq, dst_ref=ssq_recv.at[src], send_sem=ssq_send.at[dst],
-            recv_sem=ssq_recv_sem.at[src], device_id=(me, dst), device_id_type=MESH,
-        )
-
-    def each_tp(fn):
-        def step(k, _):
-            fn(lax.rem(tp + k, tp_size))
-            return 0
-
-        lax.fori_loop(1, tp_size, step, 0)
+            src_ref=ssq.at[p], dst_ref=ssq_recv.at[p, tp], send_sem=ssq_send.at[p],
+            recv_sem=ssq_recv_sem.at[p], device_id=(me, to), device_id_type=MESH,
+        )
+
+    def all_ssq(p):
+        others = ssq_recv.at[p, pl.ds(0, tp_size - 1)]
+        return pltpu.make_async_remote_copy(
+            src_ref=others, dst_ref=others, send_sem=ssq_send.at[p], recv_sem=ssq_recv_sem.at[p],
+            device_id=(me, tp), device_id_type=MESH,
+        )
 
     others = pl.ds(0, ctx_size - 1)
     all_parts = part_copy(parts.at[others], recv.at[others], right)
@@ -247,7 +256,6 @@
 
     for load in bc_loads:
         load.wait()
-    halos[0].start()
 
     bc_taps = [0.5 * convbc_ref[k : k + 1, :] for k in range(4)]
 
@@ -281,11 +289,11 @@
         def _():
             for k in range(groups * TILES):
                 x_load(k).wait()
-            halos[1].start()
-            for halo, ref in zip(halos, (bcbuf, xbuf)):
+            for halo, rim, ref in zip(halos, (bc_rim, x_rim), (bcbuf, xbuf)):
                 halo.wait_recv()
                 for k in range(ref.shape[0]):
-                    ref[k, 0:HALO] = jnp.where(me > 0, ref[k, 0:HALO].astype(F32), 0.0).astype(BF16)
+                    before = rim[:, k * LANES : (k + 1) * LANES].astype(F32)
+                    ref[k, 0:HALO] = jnp.where(me > 0, before, 0.0).astype(BF16)
 
         project(b)
         return 0
@@ -310,12 +318,11 @@
         here = start_state.at[pl.ds(mine * TILES, TILES), pl.ds(my_row, part_rows)]
         start_state[pl.ds(mine * TILES, TILES), pl.ds(my_row, part_rows)] = send[me]
 
-        def send_start(k, _):
+        def send_start(k):
             to = lax.rem(me + k, ctx_size)
             start_copy(send.at[to], here, to).start()
-            return 0
-
-        lax.fori_loop(1, ctx_size, send_start, 0)
+
+        each_other(ctx_size, send_start)
 
     batches = chunks // BATCH
 
@@ -336,49 +343,61 @@
 
         return one
 
+    def advance(u):
+        g, b = lax.div(u, batches), lax.rem(u, batches)
+        batch = [b * BATCH + k for k in range(BATCH)]
+        added = [dot(bt[c], wide(xs, g, c, slice(0, CHUNK))) for c in batch]
+
+        def follow():
+            held = jnp.where(b == 0, 0.0, state[...])
+            for c, more in zip(batch, added):
+                put(xs, g, (c, slice(CHUNK, CHUNK + n_state)), held.astype(BF16))
+                held = wide(rows_ref, g, pl.ds(c + 1, 1)) * (held + more)
+            state[...] = held
+
+        return follow
+
+    def leave(g):
+        for r in range(per_group):
+            for k in range(TILES):
+                parts[r * groups + g, k] = state[
+                    r * part_rows : (r + 1) * part_rows, k * LANES : (k + 1) * LANES
+                ].astype(BF16)
+
+        def send_part(k):
+            to = lax.rem(me // groups + k, per_group) * groups + g
+            part_copy(parts.at[to], recv.at[me], to).start()
+
+        @pl.when(mine == g)
+        def _():
+            recv[me] = parts[me]
+
+        @pl.when(mine != g)
+        def _():
+            send_part(0)
+
+        if per_group > 1:
+            each_other(per_group, send_part)
+
     def forward(u, _):
         g, b = lax.div(u, batches), lax.rem(u, batches)
         batch = [b * BATCH + k for k in range(BATCH)]
+        last_u = lax.max(u - 1, 0)
         factor = factors[pl.ds(b * BATCH, BATCH)].reshape(BATCH * CHUNK, 6 * heads)
         scales = dot(factor, wide(factor_map.at[0], g, slice(None)))
+        follow = advance(last_u)
         next_sums = tap_sums(lax.rem(u + 1, groups * batches))
-        scaled = []
         for k, c in enumerate(batch):
             value = silu_of_half(ahead[k])
             ahead[k] = next_sums(k)
             put(xconv, g, (rows_of(c),), value.astype(BF16))
-            scaled.append((value * scales[k * CHUNK : (k + 1) * CHUNK]).astype(BF16))
-            put(xs, g, (c, slice(0, CHUNK)), scaled[-1])
-        added = [dot(bt[c], value) for c, value in zip(batch, scaled)]
-        held = jnp.where(b == 0, 0.0, state[...])
-        for c, more in zip(batch, added):
-            put(xs, g, (c, slice(CHUNK, CHUNK + n_state)), held.astype(BF16))
-            held = wide(rows_ref, g, pl.ds(c + 1, 1)) * (held + more)
-        state[...] = held
-
-        @pl.when(b == batches - 1)
+            put(xs, g, (c, slice(0, CHUNK)), (value * scales[k * CHUNK : (k + 1) * CHUNK]).astype(BF16))
+        follow()
+
+        @pl.when((b == 0) & (u > 0))
         def _():
-            for r in range(per_group):
-                for k in range(TILES):
-                    parts[r * groups + g, k] = state[
-                        r * part_rows : (r + 1) * part_rows, k * LANES : (k + 1) * LANES
-                    ].astype(BF16)
-
-            @pl.when(mine == g)
-            def _():
-                recv[me] = parts[me]
-
-            def send_part(k, _):
-                to = lax.rem(me // groups + k, per_group) * groups + g
-
-                @pl.when(to != me)
-                def _():
-                    part_copy(parts.at[to], recv.at[me], to).start()
-
-                return 0
-
-            lax.fori_loop(0, per_group, send_part, 0)
-            pl.when(mine == g - 1)(carry_through)
+            leave(g - 1)
+            pl.when(mine == g - 3)(carry_through)
 
         return 0
 
@@ -386,6 +405,9 @@
     for k in range(BATCH):
         ahead[k] = first_sums(k)
     lax.fori_loop(0, groups * batches, forward, 0)
+    advance(groups * batches - 1)()
+    leave(groups - 1)
+    pl.when(mine == groups - 3)(carry_through)
 
     for k in range(groups * TILES):
         z_load(k).wait()
@@ -412,14 +434,13 @@
                 put(gate_ref, g, (rows_of(c),), (reaches[part] * gate).astype(BF16))
         return 0
 
-    half_way = chunks // PAIR // 2
-    lax.fori_loop(0, half_way, local, 0)
-    pl.when(mine == groups - 1)(carry_through)
-    lax.fori_loop(half_way, chunks // PAIR, local, 0)
+    def local_step(b, _):
+        pl.when((b >= 1) & (mine == b + (groups - 3)))(carry_through)
+        return local(b, 0)
+
+    lax.fori_loop(0, chunks // PAIR, local_step, 0)
 
     all_starts.wait_recv()
-    ssq[...] = jnp.zeros_like(ssq)
-
     def finish(b, _):
         batch = [b * PAIR + k for k in range(PAIR)]
         c_rows = c_ref[pl.ds(b * PAIR, PAIR)].reshape(PAIR * CHUNK, n_state)
@@ -438,53 +459,38 @@
             squares[c] = total[k]
         return 0
 
-    lax.fori_loop(0, chunks // PAIR, finish, 0)
-
-    def turn(b, _):
-        for c in [b * BATCH + k for k in range(BATCH)]:
-            ssq[pl.ds(c, 1), :] = jnp.sum(squares[c].T, axis=0, keepdims=True)
-        return 0
-
-    lax.fori_loop(0, chunks // BATCH, turn, 0)
-    ssq_recv[tp] = ssq[...]
-    each_tp(lambda d: ssq_copy(d, tp).start())
+    def piece(p, _):
+        for k in range(BATCH // PAIR):
+            finish(p * (BATCH // PAIR) + k, 0)
+        for k in range(BATCH):
+            ssq[p, k : k + 1, :] = jnp.sum(squares[p * BATCH + k].T, axis=0, keepdims=True)
+        ssq[p, BATCH:, :] = jnp.zeros((8 - BATCH, LANES), F32)
+        ssq_recv[p, tp] = ssq[p]
+        each_other(tp_size, lambda k: ssq_copy(p, lax.rem(tp + k, tp_size)).start())
+        return 0
+
+    lax.fori_loop(0, batches, piece, 0)
 
     for halo in halos:
         halo.wait_send()
     all_parts.wait_send()
     all_starts.wait_send()
-    each_tp(lambda s: ssq_copy(s, s).wait_recv())
-    mean = jnp.sum(ssq_recv[...], axis=0) * (1.0 / (channels * tp_size))
-    inverse[...] = lax.rsqrt(mean + 1e-5)
-    each_tp(lambda d: ssq_copy(d, d).wait_send())
-
-    def out_copy(b, lane):
-        rows = pl.ds(pl.multiple_of(b * BATCH * CHUNK, CHUNK), BATCH * CHUNK)
-        return pltpu.make_async_copy(
-            zbuf.at[lane, rows], out_hbm.at[rows, pl.ds(lane * LANES, LANES)], out_sem.at[b, lane]
-        )
 
     def norm(b, _):
-        columns = [
-            jnp.broadcast_to(inverse[pl.ds(b * BATCH + k, 1), :], (CHUNK, CHUNK)).T for k in range(BATCH)
-        ]
+        all_ssq(b).wait_recv()
+        mean = jnp.sum(ssq_recv[b], axis=0) * (1.0 / (channels * tp_size))
+        inverse = lax.rsqrt(mean + 1e-5)
+        columns = [jnp.broadcast_to(inverse[k : k + 1], (CHUNK, CHUNK)).T for k in range(BATCH)]
         for lane in range(groups * TILES):
-            gain = gain_ref[:, lane * LANES : (lane + 1) * LANES]
+            here = slice(lane * LANES, (lane + 1) * LANES)
             for k in range(BATCH):
                 at = rows_of(b * BATCH + k)
-                zbuf[lane, at] = (local_ref[lane, at] * columns[k] * gain).astype(BF16)
-        for lane in range(groups * TILES):
-            out_copy(b, lane).start()
+                out_ref[at, here] = (local_ref[lane, at] * columns[k] * gain_ref[:, here]).astype(BF16)
         return 0
 
     lax.fori_loop(0, batches, norm, 0)
-
-    def norm_done(b, _):
-        for lane in range(groups * TILES):
-            out_copy(b, lane).wait()
-        return 0
-
-    lax.fori_loop(0, batches, norm_done, 0)
+    for b in range(batches):
+        all_ssq(b).wait_send()
 
 
 def per_device(
@@ -503,13 +509,15 @@
     dma = pltpu.SemaphoreType.DMA
     return pl.pallas_call(
         functools.partial(mixer, ctx_size, tp_size, head_dim),
-        out_shape=jax.ShapeDtypeStruct((length, channels), BF16),
+        out_shape=pltpu.VMEM((length, channels), BF16),
         in_specs=[in_hbm] * 9,
-        out_specs=in_hbm,
+        out_specs=pl.BlockSpec(memory_space=pltpu.VMEM),
         scratch_shapes=[
             vmem((lanes, length + HALO, LANES), BF16),
             vmem((2, length + HALO, n_state), BF16),
             vmem((lanes, length, LANES), BF16),
+            vmem((HALO, channels), BF16),
+            vmem((HALO, 2 * n_state), BF16),
             vmem((heads, length), F32),
             vmem((heads, length), F32),
             vmem((4, channels), F32),
@@ -539,9 +547,8 @@
             vmem((lanes, length, LANES), F32),
             vmem((lanes, length, LANES), BF16),
             vmem((chunks, CHUNK, LANES), F32),
-            vmem((16, 128), F32),
-            vmem((tp_size, 16, 128), F32),
-            vmem((16, 128), F32),
+            vmem((chunks // BATCH, 8, LANES), F32),
+            vmem((chunks // BATCH, tp_size, 8, LANES), F32),
             dma((8 + 2 * lanes,)),
             dma((2,)),
             dma((2,)),
@@ -549,9 +556,8 @@
             dma((1,)),
             dma((1,)),
             dma((1,)),
-            dma((tp_size,)),
-            dma((tp_size,)),
-            dma((chunks // BATCH, lanes)),
+            dma((chunks // BATCH,)),
+            dma((chunks // BATCH,)),
         ],
         compiler_params=pltpu.CompilerParams(
             collective_id=0, has_side_effects=True, vmem_limit_bytes=56 * 1024 * 1024

time: 49 us -> 42.9 us (0.88)
  Pallas kernels: 45 us -> 41.2 us
  local copies, waits for them, and re-layouts: 3.86 us -> 1.67 us
    pallas_call x1, Pallas kernels: 45 us -> 41.2 us  [per_device(): pl.pallas_call(functools.partial(mixer, ctx_size, tp_size, head_dim), out...]
    unnamed x1, local copies, waits for them, and re-layouts: 3.86 us -> 1.67 us
where the time goes in v3:
time: 42.9 us
  Pallas kernels  41.2 us (96%)
  local copies, waits for them, and re-layouts  1.67 us (4%)
    pallas_call x1, Pallas kernels, per_device(): pl.pallas_call(functools.partial(mixer, ctx_size, tp_size, head_dim), out...  41.2 us
    unnamed x1, local copies, waits for them, and re-layouts  1.67 us

profile of v3, /device:TPU:1, one launch (start us, length us, event | category | flops | bytes accessed | tf_op | source)
XLA Modules:
  0.0 42.9 jit_solution(3643871042274601712)
XLA Ops:
  0.0 41.2 %mixer.1 = bf16[1536,1024]{1,0:T(8,128)(2,1)S(1)} custom-call(bf16[1536,1024]{1,0:T(8,128)(2,1)} %x_hbm.1, bf16[1536,256]{1,0:T(8,128)(2,1)} %bc_hbm.1, bf16[1536,1024]{1,0:T(8,128)(2,1)} %z_hbm.1, f32[4,1024]{1,0:T(4,128)} %convx_hbm.1, f32[4,256]{1,0:T(4,128)} %convbc_hbm.1, f32[16,1536]{1,0:T(8,128)} %bitcast.4, f32[16,1536]{1,0:T(8,128)} %bitcast.5, ...), custom_call_target="tpu_custom_call" | custom-call | tf_op jit(solution)/shard_map/mixer/pallas_call | solution.py:510
  41.2 1.7 %copy.11 = bf16[1536,1024]{1,0:T(8,128)(2,1)} copy(bf16[1536,1024]{1,0:T(8,128)(2,1)S(1)} %mixer.1) | data formatting | bytes 6291456

commit v4 on v3

--- a/solution.py
+++ b/solution.py
@@ -67,11 +67,14 @@
     mid = CHUNK // 2 - 1
     me = lax.axis_index("ctx")
     tp = lax.axis_index("tp")
-    mine = lax.rem(me, groups)
+    mine = lax.rem(me // 2 + me // 8, 2) * 2 + lax.rem(me, 2)
     my_row = pl.multiple_of((me // groups) * part_rows, part_rows)
 
+    def carrier(g, r):
+        return r * groups + lax.rem(g // 2 + r // 2, 2) * 2 + lax.rem(g, 2)
+
     def wide(ref, g, *at):
-        return jnp.concatenate([ref[(g * TILES + k, *at)] for k in range(TILES)], axis=-1)
+        return jnp.concatenate([ref[(g * TILES + k, *at)] if at else ref[g * TILES + k] for k in range(TILES)], axis=-1)
 
     def put(ref, g, at, value):
         for k in range(TILES):
@@ -89,25 +92,29 @@
                 (skip_hbm, skip_ref),
                 (convbc_hbm, convbc_ref),
                 (convx_hbm, convx_ref),
-                (gain_hbm, gain_ref),
+                *[
+                    (gain_hbm.at[:, pl.ds(k * LANES, LANES)], gain_ref.at[k])
+                    for k in range(groups * TILES)
+                ],
             )
         )
     ]
+    at_bc = len(small_loads)
     bc_loads = [
         pltpu.make_async_copy(
-            bc_hbm.at[:, pl.ds(k * LANES, LANES)], bcbuf.at[k, pl.ds(HALO, length)], load_sem.at[6 + k]
+            bc_hbm.at[:, pl.ds(k * LANES, LANES)], bcbuf.at[k, pl.ds(HALO, length)], load_sem.at[at_bc + k]
         )
         for k in range(2)
     ]
 
     def x_load(k):
         col = pl.ds(pl.multiple_of(k * LANES, LANES), LANES)
-        return pltpu.make_async_copy(x_hbm.at[:, col], xbuf.at[k, pl.ds(HALO, length)], load_sem.at[8 + k])
+        return pltpu.make_async_copy(x_hbm.at[:, col], xbuf.at[k, pl.ds(HALO, length)], load_sem.at[at_bc + 2 + k])
 
     def z_load(k):
         col = pl.ds(pl.multiple_of(k * LANES, LANES), LANES)
         return pltpu.make_async_copy(
-            z_hbm.at[:, col], zbuf.at[k], load_sem.at[8 + groups * TILES + k]
+            z_hbm.at[:, col], zbuf.at[k], load_sem.at[at_bc + 2 + groups * TILES + k]
         )
 
     for load in small_loads + bc_loads:
@@ -120,15 +127,13 @@
     barrier = pltpu.get_barrier_semaphore()
 
     def greet_ctx(k):
-        pl.semaphore_signal(barrier, inc=1, device_id=(lax.rem(me + k, ctx_size), tp), device_id_type=MESH)
+        pl.semaphore_signal(barrier, inc=1, device_id=(lax.rem(me + ctx_size - k, ctx_size), tp), device_id_type=MESH)
 
     def greet_tp(k):
         pl.semaphore_signal(barrier, inc=1, device_id=(me, lax.rem(tp + k, tp_size)), device_id_type=MESH)
 
     each_other(ctx_size, greet_ctx)
     each_other(tp_size, greet_tp)
-
-    pl.semaphore_wait(barrier, ctx_size + tp_size - 2)
 
     right = lax.rem(me + 1, ctx_size)
 
@@ -139,9 +144,6 @@
         )
 
     halos = [halo_copy(bc_hbm, bc_rim, 0), halo_copy(x_hbm, x_rim, 1)]
-    for halo in halos:
-        halo.start()
-
     s_at = lax.broadcasted_iota(jnp.int32, (CHUNK, CHUNK), 0)
     t_at = lax.broadcasted_iota(jnp.int32, (CHUNK, CHUNK), 1)
     upto = jnp.where(s_at <= t_at, 1.0, 0.0)
@@ -233,9 +235,21 @@
 
     def start_copy(src, dst, to):
         return pltpu.make_async_remote_copy(
-            src_ref=src, dst_ref=dst, send_sem=start_send.at[0], recv_sem=start_recv.at[0],
+            src_ref=src, dst_ref=dst, send_sem=start_send.at[0], recv_sem=start_recv.at[mine],
             device_id=(to, tp), device_id_type=MESH,
         )
+
+    def await_starts(g):
+        def some(count):
+            bytes_of = send.at[pl.ds(0, count)]
+            pltpu.make_async_remote_copy(
+                src_ref=bytes_of, dst_ref=bytes_of, send_sem=start_send.at[0], recv_sem=start_recv.at[g],
+                device_id=(right, tp), device_id_type=MESH,
+            ).wait_recv()
+
+        pl.when(mine != g)(lambda: some(per_group))
+        if per_group > 1:
+            pl.when(mine == g)(lambda: some(per_group - 1))
 
     def ssq_copy(p, to):
         return pltpu.make_async_remote_copy(
@@ -252,7 +266,6 @@
 
     others = pl.ds(0, ctx_size - 1)
     all_parts = part_copy(parts.at[others], recv.at[others], right)
-    all_starts = start_copy(send.at[others], send.at[others], right)
 
     for load in bc_loads:
         load.wait()
@@ -284,22 +297,13 @@
         for c, score in zip(batch, scores):
             scores_ref[c] = jnp.where(causal, score, 0.0).astype(BF16)
 
-    def project_step(b, _):
-        @pl.when(b == 0)
-        def _():
-            for k in range(groups * TILES):
-                x_load(k).wait()
-            for halo, rim, ref in zip(halos, (bc_rim, x_rim), (bcbuf, xbuf)):
-                halo.wait_recv()
-                for k in range(ref.shape[0]):
-                    before = rim[:, k * LANES : (k + 1) * LANES].astype(F32)
-                    ref[k, 0:HALO] = jnp.where(me > 0, before, 0.0).astype(BF16)
-
-        project(b)
-        return 0
-
-    last = chunks // BATCH - 1
-    lax.fori_loop(0, chunks // BATCH, lambda k, v: project_step(last - k, v), 0)
+    batches = chunks // BATCH
+
+    def project_step(k, _):
+        project(batches - 1 - k)
+        return 0
+
+    lax.fori_loop(0, batches - 1, project_step, 0)
 
     def carry_through():
         all_parts.wait_recv()
@@ -324,10 +328,7 @@
 
         each_other(ctx_size, send_start)
 
-    batches = chunks // BATCH
-
-    def tap_sums(u):
-        g, b = lax.div(u, batches), lax.rem(u, batches)
+    def tap_sums(g, b):
         col = pl.ds(pl.multiple_of(g * GROUP, GROUP), GROUP)
         taps = [(0.5 * convx_ref[k : k + 1, col]).astype(BF16) for k in range(4)]
         shifts = jnp.concatenate([shift_all[by] for by in range(4)] + [shift_rim[...]], axis=1)
@@ -343,29 +344,27 @@
 
         return one
 
-    def advance(u):
-        g, b = lax.div(u, batches), lax.rem(u, batches)
-        batch = [b * BATCH + k for k in range(BATCH)]
-        added = [dot(bt[c], wide(xs, g, c, slice(0, CHUNK))) for c in batch]
-
-        def follow():
-            held = jnp.where(b == 0, 0.0, state[...])
-            for c, more in zip(batch, added):
-                put(xs, g, (c, slice(CHUNK, CHUNK + n_state)), held.astype(BF16))
-                held = wide(rows_ref, g, pl.ds(c + 1, 1)) * (held + more)
-            state[...] = held
-
-        return follow
+    def scale_batch(g, b, next_sums):
+        factor = factors[pl.ds(b * BATCH, BATCH)].reshape(BATCH * CHUNK, 6 * heads)
+        scales = dot(factor, wide(factor_map.at[0], g, slice(None)))
+        scaled = []
+        for k in range(BATCH):
+            value = silu_of_half(ahead[k])
+            ahead[k] = next_sums(k)
+            put(xconv, g, (rows_of(b * BATCH + k),), value.astype(BF16))
+            scaled.append((value * scales[k * CHUNK : (k + 1) * CHUNK]).astype(BF16))
+            put(xs, g, (b * BATCH + k, slice(0, CHUNK)), scaled[-1])
+        return scaled
 
     def leave(g):
         for r in range(per_group):
             for k in range(TILES):
-                parts[r * groups + g, k] = state[
+                parts[carrier(g, r), k] = state[
                     r * part_rows : (r + 1) * part_rows, k * LANES : (k + 1) * LANES
                 ].astype(BF16)
 
         def send_part(k):
-            to = lax.rem(me // groups + k, per_group) * groups + g
+            to = carrier(g, lax.rem(me // groups + k, per_group))
             part_copy(parts.at[to], recv.at[me], to).start()
 
         @pl.when(mine == g)
@@ -379,35 +378,50 @@
         if per_group > 1:
             each_other(per_group, send_part)
 
+    later = batches - 1
+    count = groups * later
+
+    def later_at(u):
+        return lax.div(u, later), lax.rem(u, later) + 1
+
     def forward(u, _):
-        g, b = lax.div(u, batches), lax.rem(u, batches)
-        batch = [b * BATCH + k for k in range(BATCH)]
-        last_u = lax.max(u - 1, 0)
-        factor = factors[pl.ds(b * BATCH, BATCH)].reshape(BATCH * CHUNK, 6 * heads)
-        scales = dot(factor, wide(factor_map.at[0], g, slice(None)))
-        follow = advance(last_u)
-        next_sums = tap_sums(lax.rem(u + 1, groups * batches))
-        for k, c in enumerate(batch):
-            value = silu_of_half(ahead[k])
-            ahead[k] = next_sums(k)
-            put(xconv, g, (rows_of(c),), value.astype(BF16))
-            put(xs, g, (c, slice(0, CHUNK)), (value * scales[k * CHUNK : (k + 1) * CHUNK]).astype(BF16))
-        follow()
-
-        @pl.when((b == 0) & (u > 0))
-        def _():
-            leave(g - 1)
-            pl.when(mine == g - 3)(carry_through)
-
-        return 0
-
-    first_sums = tap_sums(jnp.int32(0))
+        scale_batch(*later_at(u), tap_sums(*later_at(lax.rem(u + 1, count))))
+        return 0
+
+    for k in range(groups * TILES):
+        x_load(k).wait()
+    first_sums = tap_sums(*later_at(jnp.int32(0)))
     for k in range(BATCH):
         ahead[k] = first_sums(k)
-    lax.fori_loop(0, groups * batches, forward, 0)
-    advance(groups * batches - 1)()
-    leave(groups - 1)
-    pl.when(mine == groups - 3)(carry_through)
+    lax.fori_loop(0, count // 2, forward, 0)
+    pl.semaphore_wait(barrier, ctx_size + tp_size - 2)
+    for halo in halos:
+        halo.start()
+    lax.fori_loop(count // 2, count, forward, 0)
+
+    for halo, rim, ref in zip(halos, (bc_rim, x_rim), (bcbuf, xbuf)):
+        halo.wait_recv()
+        for k in range(ref.shape[0]):
+            before = rim[:, k * LANES : (k + 1) * LANES].astype(F32)
+            ref[k, 0:HALO] = jnp.where(me > 0, before, 0.0).astype(BF16)
+    project(0)
+    first_sums = tap_sums(jnp.int32(0), 0)
+    for k in range(BATCH):
+        ahead[k] = first_sums(k)
+
+    def settle(g, _):
+        scaled = scale_batch(g, 0, tap_sums(lax.rem(g + 1, groups), 0))
+        held = jnp.zeros((n_state, GROUP), F32)
+        for c in range(chunks):
+            value = scaled[c] if c < BATCH else wide(xs, g, c, slice(0, CHUNK))
+            more = dot(bt[c], value)
+            put(xs, g, (c, slice(CHUNK, CHUNK + n_state)), held.astype(BF16))
+            held = wide(rows_ref, g, slice(c + 1, c + 2)) * (held + more)
+        state[...] = held
+        leave(g)
+        return 0
+
+    lax.fori_loop(0, groups, settle, 0)
 
     for k in range(groups * TILES):
         z_load(k).wait()
@@ -435,35 +449,45 @@
         return 0
 
     def local_step(b, _):
-        pl.when((b >= 1) & (mine == b + (groups - 3)))(carry_through)
+        pl.when(b == lax.min(chunks // PAIR // 3 + mine, chunks // PAIR - 1))(carry_through)
         return local(b, 0)
 
     lax.fori_loop(0, chunks // PAIR, local_step, 0)
 
-    all_starts.wait_recv()
-    def finish(b, _):
-        batch = [b * PAIR + k for k in range(PAIR)]
-        c_rows = c_ref[pl.ds(b * PAIR, PAIR)].reshape(PAIR * CHUNK, n_state)
-        total = [jnp.zeros((CHUNK, LANES), F32) for _ in batch]
-        for g in range(groups):
-            carried = dot(c_rows, wide(start_state, g, slice(None)))
-            for k, c in enumerate(batch):
-                gated = wide(local_ref, g, rows_of(c)) + wide(gate_ref, g, rows_of(c)).astype(F32) * carried[
-                    k * CHUNK : (k + 1) * CHUNK
-                ]
-                put(local_ref, g, (rows_of(c),), gated)
-                both = gated * gated
-                for lane in range(0, GROUP, LANES):
-                    total[k] = total[k] + both[:, lane : lane + LANES]
+    def finish(p, g):
+        batch = [p * BATCH + k for k in range(BATCH)]
+        c_rows = c_ref[pl.ds(p * BATCH, BATCH)].reshape(BATCH * CHUNK, n_state)
+        carried = dot(c_rows, wide(start_state, g, slice(None)))
+        gain = wide(gain_ref, g)
+        totals = []
         for k, c in enumerate(batch):
-            squares[c] = total[k]
-        return 0
+            reach = wide(gate_ref, g, rows_of(c)).astype(F32)
+            gated = wide(local_ref, g, rows_of(c)) + reach * carried[k * CHUNK : (k + 1) * CHUNK]
+            put(local_ref, g, (rows_of(c),), gated * gain)
+            both = gated * gated
+            total = both[:, :LANES]
+            for lane in range(LANES, GROUP, LANES):
+                total = total + both[:, lane : lane + LANES]
+            totals.append(total)
+        return batch, totals
+
+    def finish_group(g, _):
+        await_starts(g)
+
+        def step(p, _):
+            for c, total in zip(*finish(p, g)):
+                squares[c] = jnp.where(g == 0, 0.0, squares[c]) + total
+            return 0
+
+        lax.fori_loop(0, batches, step, 0)
+        return 0
+
+    lax.fori_loop(0, groups - 1, finish_group, 0)
+    await_starts(groups - 1)
 
     def piece(p, _):
-        for k in range(BATCH // PAIR):
-            finish(p * (BATCH // PAIR) + k, 0)
-        for k in range(BATCH):
-            ssq[p, k : k + 1, :] = jnp.sum(squares[p * BATCH + k].T, axis=0, keepdims=True)
+        for k, (c, total) in enumerate(zip(*finish(p, groups - 1))):
+            ssq[p, k : k + 1, :] = jnp.sum((squares[c] + total).T, axis=0, keepdims=True)
         ssq[p, BATCH:, :] = jnp.zeros((8 - BATCH, LANES), F32)
         ssq_recv[p, tp] = ssq[p]
         each_other(tp_size, lambda k: ssq_copy(p, lax.rem(tp + k, tp_size)).start())
@@ -474,18 +498,18 @@
     for halo in halos:
         halo.wait_send()
     all_parts.wait_send()
-    all_starts.wait_send()
+    start_copy(send.at[others], send.at[others], right).wait_send()
 
     def norm(b, _):
         all_ssq(b).wait_recv()
         mean = jnp.sum(ssq_recv[b], axis=0) * (1.0 / (channels * tp_size))
         inverse = lax.rsqrt(mean + 1e-5)
-        columns = [jnp.broadcast_to(inverse[k : k + 1], (CHUNK, CHUNK)).T for k in range(BATCH)]
-        for lane in range(groups * TILES):
-            here = slice(lane * LANES, (lane + 1) * LANES)
-            for k in range(BATCH):
-                at = rows_of(b * BATCH + k)
-                out_ref[at, here] = (local_ref[lane, at] * columns[k] * gain_ref[:, here]).astype(BF16)
+        for k in range(BATCH):
+            at = rows_of(b * BATCH + k)
+            column = jnp.broadcast_to(inverse[k : k + 1], (CHUNK, CHUNK)).T
+            for lane in range(groups * TILES):
+                here = slice(lane * LANES, (lane + 1) * LANES)
+                out_ref[at, here] = (local_ref[lane, at] * column).astype(BF16)
         return 0
 
     lax.fori_loop(0, batches, norm, 0)
@@ -523,7 +547,7 @@
             vmem((4, channels), F32),
             vmem((4, 2 * n_state), F32),
             vmem((1, heads), F32),
-            vmem((1, channels), F32),
+            vmem((lanes, 1, LANES), F32),
             vmem((3 * heads, channels), BF16),
             vmem((3, lanes, 6 * heads, LANES), BF16),
             vmem((3 * CHUNK, CHUNK + HALO), BF16),
@@ -549,13 +573,13 @@
             vmem((chunks, CHUNK, LANES), F32),
             vmem((chunks // BATCH, 8, LANES), F32),
             vmem((chunks // BATCH, tp_size, 8, LANES), F32),
-            dma((8 + 2 * lanes,)),
+            dma((7 + 3 * lanes,)),
             dma((2,)),
             dma((2,)),
             dma((1,)),
             dma((1,)),
             dma((1,)),
-            dma((1,)),
+            dma((groups,)),
             dma((chunks // BATCH,)),
             dma((chunks // BATCH,)),
         ],

time: 42.9 us -> 40.6 us (0.946)
  Pallas kernels: 41.2 us -> 38.8 us
    pallas_call x1, Pallas kernels: 41.2 us -> 38.8 us  [per_device(): pl.pallas_call(functools.partial(mixer, ctx_size, tp_size, head_dim), out...]
where the time goes in v4:
time: 40.6 us; the launch traced here: 40.5 us
  Pallas kernels  38.8 us (96%)
  local copies, waits for them, and re-layouts  1.67 us (4%)
    pallas_call x1, Pallas kernels, per_device(): pl.pallas_call(functools.partial(mixer, ctx_size, tp_size, head_dim), out...  38.8 us
    unnamed x1, local copies, waits for them, and re-layouts  1.67 us

profile of v4, /device:TPU:1, one launch (start us, length us, event | category | flops | bytes accessed | tf_op | source)
XLA Modules:
  0.0 40.5 jit_solution(8605142568978015957)
XLA Ops:
  0.0 38.8 %mixer.1 = bf16[1536,1024]{1,0:T(8,128)(2,1)S(1)} custom-call(bf16[1536,1024]{1,0:T(8,128)(2,1)} %x_hbm.1, bf16[1536,256]{1,0:T(8,128)(2,1)} %bc_hbm.1, bf16[1536,1024]{1,0:T(8,128)(2,1)} %z_hbm.1, f32[4,1024]{1,0:T(4,128)} %convx_hbm.1, f32[4,256]{1,0:T(4,128)} %convbc_hbm.1, f32[16,1536]{1,0:T(8,128)} %bitcast.4, f32[16,1536]{1,0:T(8,128)} %bitcast.5, ...), custom_call_target="tpu_custom_call" | custom-call | tf_op jit(solution)/shard_map/mixer/pallas_call | solution.py:534
  38.8 1.7 %copy.11 = bf16[1536,1024]{1,0:T(8,128)(2,1)} copy(bf16[1536,1024]{1,0:T(8,128)(2,1)S(1)} %mixer.1) | data formatting | bytes 6291456

commit v5 on v4

--- a/solution.py
+++ b/solution.py
@@ -168,10 +168,9 @@
         at = lax.broadcasted_iota(jnp.int32, (CHUNK, width), 1)
         return jnp.where(to + (before - by) == at, 1.0, 0.0).astype(BF16)
 
-    for by in range(4):
-        shift_all[by] = shift(by, CHUNK, 0)
-        if by > 0:
-            shift_one[(by - 1) * CHUNK : by * CHUNK, :] = shift(by, CHUNK + HALO, HALO)
+    for by in range(1, 4):
+        shift_all[by - 1] = shift(by, CHUNK, 0)
+        shift_one[(by - 1) * CHUNK : by * CHUNK, :] = shift(by, CHUNK + HALO, HALO)
     halo_to = lax.broadcasted_iota(jnp.int32, (CHUNK, 3 * HALO), 0)
     halo_at = lax.broadcasted_iota(jnp.int32, (CHUNK, 3 * HALO), 1)
     halo_hit = halo_to < 0
@@ -211,7 +210,7 @@
         return before, windows
 
     none = jnp.zeros((heads, CHUNK), F32)
-    _, windows = lax.fori_loop(0, chunks // BATCH, decays, (none, none))
+    _, windows = lax.fori_loop(0, chunks // BATCH, decays, (none, none), unroll=True)
     head_rows = jnp.exp(windows).T[:16]
     lam_row = jnp.concatenate(split3(head_rows[15:16]) + (jnp.zeros((1, LANES - 3 * heads), BF16),), axis=1)
     lam_tile = jnp.broadcast_to(lam_row.astype(F32), (part_rows, LANES)).astype(BF16)
@@ -272,38 +271,42 @@
 
     bc_taps = [0.5 * convbc_ref[k : k + 1, :] for k in range(4)]
 
-    def project(b):
-        batch = [b * BATCH + k for k in range(BATCH)]
-        blocks, moved = [], []
-        for c in batch:
-            rows = pl.ds(pl.multiple_of(c * CHUNK, CHUNK), CHUNK + HALO)
-            blocks.append(jnp.concatenate((bcbuf[0, rows], bcbuf[1, rows]), axis=1))
-        for block in blocks:
-            moved.append(dot(shift_one[...], block))
-        turned, c_rows = [], []
-        for c, block, move in zip(batch, blocks, moved):
-            half = bc_taps[3] * block[HALO:].astype(F32)
+    def project(side, b):
+        part = slice(side * n_state, (side + 1) * n_state)
+        blocks = [
+            bcbuf[side, pl.ds(pl.multiple_of((b * BATCH + k) * CHUNK, CHUNK), CHUNK + HALO)] for k in range(BATCH)
+        ]
+        moved = [dot(shift_one[...], block) for block in blocks]
+        results = []
+        for block, move in zip(blocks, moved):
+            half = bc_taps[3][:, part] * block[HALO:].astype(F32)
             for by in range(1, 4):
-                half = half + bc_taps[3 - by] * move[(by - 1) * CHUNK : by * CHUNK]
-            both = silu_of_half(half).astype(BF16)
-            c_rows.append(both[:, n_state:])
-            turned.append(both[:, :n_state].T)
-            bt[c] = turned[-1]
-            c_ref[c] = c_rows[-1]
+                half = half + bc_taps[3 - by][:, part] * move[(by - 1) * CHUNK : by * CHUNK]
+            results.append(silu_of_half(half).astype(BF16))
+        return results
+
+    def project_b(b):
+        for k, value in enumerate(project(0, b)):
+            bt[b * BATCH + k] = value.T
+
+    def project_c(b, _):
+        values = project(1, b)
         causal = lax.broadcasted_iota(jnp.int32, (CHUNK, CHUNK), 0) >= lax.broadcasted_iota(
             jnp.int32, (CHUNK, CHUNK), 1
         )
-        scores = [dot(c_row, b_turned) for c_row, b_turned in zip(c_rows, turned)]
-        for c, score in zip(batch, scores):
-            scores_ref[c] = jnp.where(causal, score, 0.0).astype(BF16)
+        scores = [dot(value, bt[b * BATCH + k]) for k, value in enumerate(values)]
+        for k, value in enumerate(values):
+            c_ref[b * BATCH + k] = value
+            scores_ref[b * BATCH + k] = jnp.where(causal, scores[k], 0.0).astype(BF16)
+        return 0
 
     batches = chunks // BATCH
 
     def project_step(k, _):
-        project(batches - 1 - k)
-        return 0
-
-    lax.fori_loop(0, batches - 1, project_step, 0)
+        project_b(batches - 1 - k)
+        return 0
+
+    lax.fori_loop(0, batches - 1, project_step, 0, unroll=True)
 
     def carry_through():
         all_parts.wait_recv()
@@ -323,24 +326,23 @@
         start_state[pl.ds(mine * TILES, TILES), pl.ds(my_row, part_rows)] = send[me]
 
         def send_start(k):
-            to = lax.rem(me + k, ctx_size)
+            far_first = lax.rem(k + ctx_size // 3, ctx_size - 1) + 1
+            to = lax.rem(me + far_first, ctx_size)
             start_copy(send.at[to], here, to).start()
 
         each_other(ctx_size, send_start)
 
     def tap_sums(g, b):
         col = pl.ds(pl.multiple_of(g * GROUP, GROUP), GROUP)
-        taps = [(0.5 * convx_ref[k : k + 1, col]).astype(BF16) for k in range(4)]
-        shifts = jnp.concatenate([shift_all[by] for by in range(4)] + [shift_rim[...]], axis=1)
+        taps = [(0.5 * convx_ref[k : k + 1, col]).astype(BF16) for k in range(3)]
+        shifts = jnp.concatenate([shift_all[by] for by in range(3)] + [shift_rim[...]], axis=1)
 
         def one(k):
             at = pl.multiple_of((b * BATCH + k) * CHUNK, CHUNK)
             block = wide(xbuf, g, pl.ds(at, CHUNK + HALO))
             terms = [block * taps[3 - by] for by in range(1, 4)]
-            stacked = jnp.concatenate(
-                [block[HALO:] * taps[3]] + [term[HALO:] for term in terms] + [term[:HALO] for term in terms], axis=0
-            )
-            return dot(shifts, stacked)
+            stacked = jnp.concatenate([term[HALO:] for term in terms] + [term[:HALO] for term in terms], axis=0)
+            return dot(shifts, stacked) + 0.5 * convx_ref[3:4, col] * block[HALO:].astype(F32)
 
         return one
 
@@ -393,18 +395,18 @@
     first_sums = tap_sums(*later_at(jnp.int32(0)))
     for k in range(BATCH):
         ahead[k] = first_sums(k)
-    lax.fori_loop(0, count // 2, forward, 0)
+    lax.fori_loop(0, count // 2, forward, 0, unroll=2)
     pl.semaphore_wait(barrier, ctx_size + tp_size - 2)
     for halo in halos:
         halo.start()
-    lax.fori_loop(count // 2, count, forward, 0)
+    lax.fori_loop(count // 2, count, forward, 0, unroll=2)
 
     for halo, rim, ref in zip(halos, (bc_rim, x_rim), (bcbuf, xbuf)):
         halo.wait_recv()
         for k in range(ref.shape[0]):
             before = rim[:, k * LANES : (k + 1) * LANES].astype(F32)
             ref[k, 0:HALO] = jnp.where(me > 0, before, 0.0).astype(BF16)
-    project(0)
+    project_b(0)
     first_sums = tap_sums(jnp.int32(0), 0)
     for k in range(BATCH):
         ahead[k] = first_sums(k)
@@ -423,6 +425,7 @@
 
     lax.fori_loop(0, groups, settle, 0)
 
+    lax.fori_loop(0, batches, project_c, 0)
     for k in range(groups * TILES):
         z_load(k).wait()
 
@@ -490,7 +493,9 @@
             ssq[p, k : k + 1, :] = jnp.sum((squares[c] + total).T, axis=0, keepdims=True)
         ssq[p, BATCH:, :] = jnp.zeros((8 - BATCH, LANES), F32)
         ssq_recv[p, tp] = ssq[p]
-        each_other(tp_size, lambda k: ssq_copy(p, lax.rem(tp + k, tp_size)).start())
+        each_other(
+            tp_size, lambda k: ssq_copy(p, lax.rem(tp + lax.rem(k + 1, tp_size - 1) + 1, tp_size)).start()
+        )
         return 0
 
     lax.fori_loop(0, batches, piece, 0)
@@ -551,7 +556,7 @@
             vmem((3 * heads, channels), BF16),
             vmem((3, lanes, 6 * heads, LANES), BF16),
             vmem((3 * CHUNK, CHUNK + HALO), BF16),
-            vmem((4, CHUNK, CHUNK), BF16),
+            vmem((3, CHUNK, CHUNK), BF16),
             vmem((CHUNK, 3 * HALO), BF16),
             vmem((3, CHUNK, CHUNK), BF16),
             vmem((chunks, CHUNK, 6 * heads), BF16),

time: 40.6 us -> 39 us (0.961)
  Pallas kernels: 38.8 us -> 37.2 us
    pallas_call x1, Pallas kernels: 38.8 us -> 37.2 us  [per_device(): pl.pallas_call(functools.partial(mixer, ctx_size, tp_size, head_dim), out...]
where the time goes in v5:
time: 39 us; the launch traced here: 38.9 us
  Pallas kernels  37.2 us (95%)
  local copies, waits for them, and re-layouts  1.67 us (4%)
    pallas_call x1, Pallas kernels, per_device(): pl.pallas_call(functools.partial(mixer, ctx_size, tp_size, head_dim), out...  37.2 us
    unnamed x1, local copies, waits for them, and re-layouts  1.67 us

profile of v5, /device:TPU:1, one launch (start us, length us, event | category | flops | bytes accessed | tf_op | source)
XLA Modules:
  0.0 38.9 jit_solution(1086989545013792725)
XLA Ops:
  0.0 37.2 %mixer.1 = bf16[1536,1024]{1,0:T(8,128)(2,1)S(1)} custom-call(bf16[1536,1024]{1,0:T(8,128)(2,1)} %x_hbm.1, bf16[1536,256]{1,0:T(8,128)(2,1)} %bc_hbm.1, bf16[1536,1024]{1,0:T(8,128)(2,1)} %z_hbm.1, f32[4,1024]{1,0:T(4,128)} %convx_hbm.1, f32[4,256]{1,0:T(4,128)} %convbc_hbm.1, f32[16,1536]{1,0:T(8,128)} %bitcast.4, f32[16,1536]{1,0:T(8,128)} %bitcast.5, ...), custom_call_target="tpu_custom_call" | custom-call | tf_op jit(solution)/shard_map/mixer/pallas_call | solution.py:539
  37.2 1.7 %copy.11 = bf16[1536,1024]{1,0:T(8,128)(2,1)} copy(bf16[1536,1024]{1,0:T(8,128)(2,1)S(1)} %mixer.1) | data formatting | bytes 6291456

commit v6 on v5

--- a/solution.py
+++ b/solution.py
@@ -132,8 +132,10 @@
     def greet_tp(k):
         pl.semaphore_signal(barrier, inc=1, device_id=(me, lax.rem(tp + k, tp_size)), device_id_type=MESH)
 
-    each_other(ctx_size, greet_ctx)
-    each_other(tp_size, greet_tp)
+    for k in range(1, ctx_size):
+        greet_ctx(k)
+    for k in range(1, tp_size):
+        greet_tp(k)
 
     right = lax.rem(me + 1, ctx_size)
 
@@ -325,12 +327,10 @@
         here = start_state.at[pl.ds(mine * TILES, TILES), pl.ds(my_row, part_rows)]
         start_state[pl.ds(mine * TILES, TILES), pl.ds(my_row, part_rows)] = send[me]
 
-        def send_start(k):
-            far_first = lax.rem(k + ctx_size // 3, ctx_size - 1) + 1
+        for k in range(1, ctx_size):
+            far_first = (k + ctx_size // 3) % (ctx_size - 1) + 1
             to = lax.rem(me + far_first, ctx_size)
             start_copy(send.at[to], here, to).start()
-
-        each_other(ctx_size, send_start)
 
     def tap_sums(g, b):
         col = pl.ds(pl.multiple_of(g * GROUP, GROUP), GROUP)
@@ -352,7 +352,8 @@
         scaled = []
         for k in range(BATCH):
             value = silu_of_half(ahead[k])
-            ahead[k] = next_sums(k)
+            if next_sums is not None:
+                ahead[k] = next_sums(k)
             put(xconv, g, (rows_of(b * BATCH + k),), value.astype(BF16))
             scaled.append((value * scales[k * CHUNK : (k + 1) * CHUNK]).astype(BF16))
             put(xs, g, (b * BATCH + k, slice(0, CHUNK)), scaled[-1])
@@ -377,8 +378,8 @@
         def _():
             send_part(0)
 
-        if per_group > 1:
-            each_other(per_group, send_part)
+        for k in range(1, per_group):
+            send_part(k)
 
     later = batches - 1
     count = groups * later
@@ -411,8 +412,8 @@
     for k in range(BATCH):
         ahead[k] = first_sums(k)
 
-    def settle(g, _):
-        scaled = scale_batch(g, 0, tap_sums(lax.rem(g + 1, groups), 0))
+    def settle(g):
+        scaled = scale_batch(g, 0, tap_sums(g + 1, 0) if g + 1 < groups else None)
         held = jnp.zeros((n_state, GROUP), F32)
         for c in range(chunks):
             value = scaled[c] if c < BATCH else wide(xs, g, c, slice(0, CHUNK))
@@ -420,10 +421,10 @@
             put(xs, g, (c, slice(CHUNK, CHUNK + n_state)), held.astype(BF16))
             held = wide(rows_ref, g, slice(c + 1, c + 2)) * (held + more)
         state[...] = held
-        leave(g)
-        return 0
-
-    lax.fori_loop(0, groups, settle, 0)
+        leave(jnp.int32(g))
+
+    for g in range(groups):
+        settle(g)
 
     lax.fori_loop(0, batches, project_c, 0)
     for k in range(groups * TILES):
@@ -452,7 +453,7 @@
         return 0
 
     def local_step(b, _):
-        pl.when(b == lax.min(chunks // PAIR // 3 + mine, chunks // PAIR - 1))(carry_through)
+        pl.when(b == lax.min(1 + mine, chunks // PAIR - 1))(carry_through)
         return local(b, 0)
 
     lax.fori_loop(0, chunks // PAIR, local_step, 0)
@@ -493,12 +494,11 @@
             ssq[p, k : k + 1, :] = jnp.sum((squares[c] + total).T, axis=0, keepdims=True)
         ssq[p, BATCH:, :] = jnp.zeros((8 - BATCH, LANES), F32)
         ssq_recv[p, tp] = ssq[p]
-        each_other(
-            tp_size, lambda k: ssq_copy(p, lax.rem(tp + lax.rem(k + 1, tp_size - 1) + 1, tp_size)).start()
-        )
-        return 0
-
-    lax.fori_loop(0, batches, piece, 0)
+        for k in range(1, tp_size):
+            ssq_copy(p, lax.rem(tp + (k + 1) % (tp_size - 1) + 1, tp_size)).start()
+        return 0
+
+    lax.fori_loop(0, batches, piece, 0, unroll=True)
 
     for halo in halos:
         halo.wait_send()

time: 39 us -> 38.5 us (0.987)
  Pallas kernels: 37.2 us -> 36.8 us
    pallas_call x1, Pallas kernels: 37.2 us -> 36.8 us  [per_device(): pl.pallas_call(functools.partial(mixer, ctx_size, tp_size, head_dim), out...]
where the time goes in v6:
time: 38.5 us
  Pallas kernels  36.8 us (96%)
  local copies, waits for them, and re-layouts  1.67 us (4%)
    pallas_call x1, Pallas kernels, per_device(): pl.pallas_call(functools.partial(mixer, ctx_size, tp_size, head_dim), out...  36.8 us
    unnamed x1, local copies, waits for them, and re-layouts  1.67 us

profile of v6, /device:TPU:1, one launch (start us, length us, event | category | flops | bytes accessed | tf_op | source)
XLA Modules:
  0.0 38.5 jit_solution(6779517929044184246)
XLA Ops:
  0.0 36.8 %mixer.1 = bf16[1536,1024]{1,0:T(8,128)(2,1)S(1)} custom-call(bf16[1536,1024]{1,0:T(8,128)(2,1)} %x_hbm.1, bf16[1536,256]{1,0:T(8,128)(2,1)} %bc_hbm.1, bf16[1536,1024]{1,0:T(8,128)(2,1)} %z_hbm.1, f32[4,1024]{1,0:T(4,128)} %convx_hbm.1, f32[4,256]{1,0:T(4,128)} %convbc_hbm.1, f32[16,1536]{1,0:T(8,128)} %bitcast.4, f32[16,1536]{1,0:T(8,128)} %bitcast.5, ...), custom_call_target="tpu_custom_call" | custom-call | tf_op jit(solution)/shard_map/mixer/pallas_call | solution.py:539
  36.8 1.7 %copy.11 = bf16[1536,1024]{1,0:T(8,128)(2,1)} copy(bf16[1536,1024]{1,0:T(8,128)(2,1)S(1)} %mixer.1) | data formatting | bytes 6291456

commit v7 on v5

--- a/solution.py
+++ b/solution.py
@@ -395,11 +395,11 @@
     first_sums = tap_sums(*later_at(jnp.int32(0)))
     for k in range(BATCH):
         ahead[k] = first_sums(k)
-    lax.fori_loop(0, count // 2, forward, 0, unroll=2)
+    lax.fori_loop(0, count // 4, forward, 0, unroll=2)
     pl.semaphore_wait(barrier, ctx_size + tp_size - 2)
     for halo in halos:
         halo.start()
-    lax.fori_loop(count // 2, count, forward, 0, unroll=2)
+    lax.fori_loop(count // 4, count, forward, 0, unroll=2)
 
     for halo, rim, ref in zip(halos, (bc_rim, x_rim), (bcbuf, xbuf)):
         halo.wait_recv()
@@ -498,7 +498,7 @@
         )
         return 0
 
-    lax.fori_loop(0, batches, piece, 0)
+    lax.fori_loop(0, batches, piece, 0, unroll=True)
 
     for halo in halos:
         halo.wait_send()

time: 39 us -> 37.8 us (0.969)
  Pallas kernels: 37.2 us -> 36.1 us
    pallas_call x1, Pallas kernels: 37.2 us -> 36.1 us  [per_device(): pl.pallas_call(functools.partial(mixer, ctx_size, tp_size, head_dim), out...]
where the time goes in v7:
time: 37.8 us
  Pallas kernels  36.1 us (96%)
  local copies, waits for them, and re-layouts  1.67 us (4%)
    pallas_call x1, Pallas kernels, per_device(): pl.pallas_call(functools.partial(mixer, ctx_size, tp_size, head_dim), out...  36.1 us
    unnamed x1, local copies, waits for them, and re-layouts  1.67 us

profile of v7, /device:TPU:1, one launch (start us, length us, event | category | flops | bytes accessed | tf_op | source)
XLA Modules:
  0.0 37.8 jit_solution(11354292032814000114)
XLA Ops:
  0.0 36.1 %mixer.1 = bf16[1536,1024]{1,0:T(8,128)(2,1)S(1)} custom-call(bf16[1536,1024]{1,0:T(8,128)(2,1)} %x_hbm.1, bf16[1536,256]{1,0:T(8,128)(2,1)} %bc_hbm.1, bf16[1536,1024]{1,0:T(8,128)(2,1)} %z_hbm.1, f32[4,1024]{1,0:T(4,128)} %convx_hbm.1, f32[4,256]{1,0:T(4,128)} %convbc_hbm.1, f32[16,1536]{1,0:T(8,128)} %bitcast.4, f32[16,1536]{1,0:T(8,128)} %bitcast.5, ...), custom_call_target="tpu_custom_call" | custom-call | tf_op jit(solution)/shard_map/mixer/pallas_call | solution.py:539
  36.1 1.7 %copy.11 = bf16[1536,1024]{1,0:T(8,128)(2,1)} copy(bf16[1536,1024]{1,0:T(8,128)(2,1)S(1)} %mixer.1) | data formatting | bytes 6291456
